TPU v7x, 512 devices: a whole 4x8x8 slice. The times are simulated.
512 devices in a mesh: team: 4 (over y_hi), blk: 128 (over x, y_lo, z, core).
Axes of the slice: x: 4, y: 8 (y_hi: 4, y_lo: 2; y = y_hi * 2 + y_lo), z: 8, core: 2. Of those that a mesh axis runs over, the one named last changes fastest.
Arguments:
- position: float32 [3, 131072], P(None, ('team', 'blk')), may hold values from -6 to 6
- velocity: float32 [3, 131072], P(None, ('team', 'blk')), may hold values from -6 to 6
- old_accel: float32 [3, 131072], P(None, ('team', 'blk')), may hold values from -6 to 6
- old_jerk: float32 [3, 131072], P(None, ('team', 'blk')), may hold values from -6 to 6
- mass: float32 [131072], P(('team', 'blk')), may hold values from 1.5258789e-06 to 3.8146973e-05
- elapsed: float32 [131072], P(('team', 'blk')), may hold values from 0.0625 to 0.5
- active_slot: int32 [16384], P('blk'), may hold values from 0 to 255, as said below
- active_owner: int32 [16384], P('blk'), may hold values from 0 to 3
Outputs:
- phase: float32 [6, 16384], P(None, 'blk')
- force: float32 [6, 16384], P(None, 'blk')
- higher: float32 [6, 16384], P(None, 'blk')
Inputs may be any that keep to these rules, and one draw needn't show every extreme that they name: Within each block of 128 active entries the pairs (active_owner, active_slot) are all different; slot 255 of owner 3 and slot 0 of owner 0 are active in every block.
All inputs are finite; a program needn't handle non-finite values.
Results may differ from a plain program's by a relative error of at most 0.0003.
Values sent between devices are 32-bit elements; how exact they have to be, the bound alone decides.
No kernel may reach another device: no remote copies, remote signals or barrier semaphores. Data moves between devices by JAX's collectives and lax.ppermute only.
A program may use at most 64 MiB of HBM per device.

v0:
```python
import jax
import jax.numpy as jnp
from jax import lax
from jax.sharding import PartitionSpec as P

SOFTEN2 = 0.0001


def predict(x, v, a, j, h):
    xp = x + h * (v + h * (a / 2.0 + h * j / 6.0))
    vp = v + h * (a + h * j / 2.0)
    return (xp, vp)


def pair_block(ipack, jpack):
    dx = jpack[0:3, None, :] - ipack[0:3, :, None]
    dv = jpack[3:6, None, :] - ipack[3:6, :, None]
    r2 = jnp.sum(dx * dx, axis=0) + SOFTEN2
    inv = 1.0 / jnp.sqrt(r2)
    weight = jpack[6][None, :] * inv * inv * inv
    rv = 3.0 * jnp.sum(dx * dv, axis=0) / r2
    acc = jnp.sum(weight * dx, axis=2)
    jerk = jnp.sum(weight * (dv - rv * dx), axis=2)
    return jnp.concatenate([acc, jerk], axis=0)


def correct(own, total):
    x0, v0, a0, j0, dt = (own[0:3], own[3:6], own[6:9], own[9:12], own[12:13])
    a1, j1 = (total[0:3], total[3:6])
    v1 = v0 + (a0 + a1) * dt / 2.0 + (j0 - j1) * dt * dt / 12.0
    x1 = x0 + (v0 + v1) * dt / 2.0 + (a0 - a1) * dt * dt / 12.0
    snap = -6.0 * (a0 - a1) - dt * (4.0 * j0 + 2.0 * j1)
    crackle = 12.0 * (a0 - a1) + 6.0 * dt * (j0 + j1)
    return (jnp.concatenate([x1, v1], 0), total, jnp.concatenate([snap, crackle], 0))


def shards(position, velocity, old_accel, old_jerk, mass, elapsed, active_slot, active_owner):
    members = position.shape[1]
    actives = active_slot.shape[0]
    team_index = lax.axis_index("team")
    state = jnp.concatenate([position, velocity, old_accel, old_jerk, elapsed[None, :]], axis=0)
    column_ids = lax.broadcasted_iota(jnp.int32, (actives, members), 1)
    selector = (
        (active_slot[:, None] == column_ids) & (active_owner[:, None] == team_index)
    ).astype(jnp.float32)
    chosen = jnp.einsum("cj,aj->ca", state, selector, precision=lax.Precision.HIGHEST)
    own = lax.psum(chosen, "team")
    xi, vi = predict(own[0:3], own[3:6], own[6:9], own[9:12], own[12:13])
    ipack = jnp.concatenate([xi, vi], axis=0)
    xp, vp = predict(position, velocity, old_accel, old_jerk, elapsed[None, :])
    jpack = jnp.concatenate([xp, vp, mass[None, :]], axis=0)
    piece = lax.all_gather(jpack, "blk", axis=1, tiled=True)
    width = piece.shape[1]
    step = 512

    def one_step(k, acc):
        sliced = lax.dynamic_slice_in_dim(piece, k * step, step, 1)
        return acc + pair_block(ipack, sliced)

    partial_value = lax.fori_loop(0, width // step, one_step, jnp.zeros((6, actives), jnp.float32))
    total = lax.psum(partial_value, "team")
    return correct(own, total)


def solution(mesh):
    placed = (
        P(None, ("team", "blk")),
        P(None, ("team", "blk")),
        P(None, ("team", "blk")),
        P(None, ("team", "blk")),
        P(("team", "blk")),
        P(("team", "blk")),
        P("blk"),
        P("blk"),
    )
    return jax.shard_map(
        shards,
        mesh=mesh,
        in_specs=placed,
        out_specs=(P(None, "blk"), P(None, "blk"), P(None, "blk")),
        check_vma=False,
    )
```

profile of v0, /device:TPU:1, one launch (start us, length us, event | category | flops | bytes accessed | tf_op | source)
XLA Modules:
  0.0 254.0 jit_solution(9529318480873149719)
XLA Ops:
  0.6 0.7 copy-done.5
  1.3 2.2 concatenate.19
  3.5 0.7 copy-done.7
  4.2 0.6 copy-done.8
  5.0 11.8 %psum.14 = f32[13,128]{1,0:T(8,128)S(1)} all-reduce(f32[13,128]{1,0:T(8,128)S(1)} %fusion.6), channel_id=1, replica_groups=mesh['team'=4,'blk'=128] {'team'}, use_global_device_ids=true, to_apply=%region_0.0 | all-reduce | flops 1664 | bytes 13312 | tf_op jit(solution)/shard_map/psum | solution.py:47
  17.0 0.6 copy-done
  17.7 0.7 copy-done.6
  18.3 167.4 %all_gather.3 = f32[7,32768]{1,0:T(8,128)S(1)} all-gather(f32[7,256]{1,0:T(8,128)S(1)} %pad_maximum_fusion), channel_id=1, replica_groups=mesh['team'=4,'blk'=128] {'blk'}, dimensions={1}, use_global_device_ids=true | all-gather | bytes 924672 | tf_op jit(solution)/shard_map/all_gather | solution.py:52
  185.8 58.3 %while.14 = (s32[]{:T(128)}, f32[6,128]{1,0:T(8,128)S(1)}, f32[7,32768]{1,0:T(8,128)S(1)}, f32[3,128]{1,0:T(4,128)S(1)}, f32[3,128]{1,0:T(4,128)S(1)}, /*index=5...) while((s32[]{:T(128)}, f32[6,128]{1,0:T(8,128)S(1)}, ...), condition=%wide.region_6.0_spmd.clone, body=%wide.region_1.0_spmd.clone.sunk | while | flops 3016201 | bytes 2171081 | solution.py:60
  186.2 0.4 fusion.17
  187.1 0.4 fusion.17
  188.1 0.4 fusion.17
  189.0 0.4 fusion.17
  189.9 0.4 fusion.17
  191.7 0.4 fusion.17
  192.6 0.4 fusion.17
  193.5 0.4 fusion.17
  194.4 0.4 fusion.17
  195.3 0.4 fusion.17
  196.3 0.4 fusion.17
  197.2 0.4 fusion.17
  198.1 0.4 fusion.17
  199.0 0.4 fusion.17
  199.9 0.4 fusion.17
  200.8 0.4 fusion.17
  201.7 0.4 fusion.17
  202.6 0.4 fusion.17
  203.6 0.4 fusion.17
  204.5 0.4 fusion.17
  205.4 0.4 fusion.17
  206.3 0.4 fusion.17
  207.2 0.4 fusion.17
  209.0 0.4 fusion.17
  209.9 0.4 fusion.17
  210.8 0.4 fusion.17
  211.8 0.4 fusion.17
  212.7 0.4 fusion.17
  213.6 0.4 fusion.17
  214.5 0.4 fusion.17
  215.4 0.4 fusion.17
  216.3 0.4 fusion.17
  217.2 0.4 fusion.17
  218.1 0.4 fusion.17
  219.1 0.4 fusion.17
  220.0 0.4 fusion.17
  244.1 8.8 %psum.15 = f32[6,128]{1,0:T(8,128)S(1)} all-reduce(f32[6,128]{1,0:T(8,128)S(1)} %get-tuple-element.97), channel_id=1, replica_groups=mesh['team'=4,'blk'=128] {'team'}, use_global_device_ids=true, to_apply=%region_7.0 | all-reduce | flops 768 | bytes 6144 | tf_op jit(solution)/shard_map/psum | solution.py:61
  252.9 0.6 copy-done.4
  253.4 0.6 pad_maximum_fusion.1
  (368 shorter events, 41.5 us)
Async XLA Ops:
  0.6 0.7 copy-start.5
  3.5 0.7 copy-start.7
  4.2 0.7 copy-start.8
  16.9 0.7 copy-start
  16.9 0.7 copy-start.1
  16.9 0.7 copy-start.2
  16.9 0.7 copy-start.3
  17.6 0.7 copy-start.6
  252.8 0.6 copy-start.4
where the time goes:
time: 254 us
  blocking collectives  188 us (74%)
  other arithmetic  45.9 us (18%)
  local copies, waits for them, and re-layouts  16.6 us (7%)
  loops' own time  2.64 us (1%)
    all_gather x1, blocking collectives, shards(): piece = lax.all_gather(jpack, 'blk', axis=1, tiled=True)  167 us
    reduce_sum x64, other arithmetic, pair_block(): acc = jnp.sum(weight * dx, axis=2)  25.7 us
    reduce_sum x64, other arithmetic, pair_block(): r2 = jnp.sum(dx * dx, axis=0) + SOFTEN2  13.8 us
    psum x1, blocking collectives, shards(): own = lax.psum(chosen, 'team')  11.8 us
    psum x1, blocking collectives, shards(): total = lax.psum(partial_value, 'team')  8.75 us
    slice x64, local copies, waits for them, and re-layouts, pair_block(): weight = jpack[6][None, :] * inv * inv * inv  5.22 us
    slice x64, local copies, waits for them, and re-layouts, pair_block(): dv = jpack[3:6, None, :] - ipack[3:6, :, None]  5.22 us

commit v1 on v0

v1 whole, which is shorter than its diff:
```python
import functools
import jax
import jax.numpy as jnp
from jax import lax
from jax.experimental import pallas as pl
from jax.experimental.pallas import tpu as pltpu
from jax.sharding import Mesh, PartitionSpec as P

SOFTEN2 = 0.0001
N_X, N_YLO, N_Z, N_CORE = 4, 2, 8, 2
LANES = 128
GATHER = ("x", "z")
REDUCE = ("team", "y", "core")


def predict(x, v, a, j, h):
    xp = x + h * (v + h * (a / 2.0 + h * j / 6.0))
    vp = v + h * (a + h * j / 2.0)
    return (xp, vp)


def pack_kernel(x_ref, v_ref, a_ref, j_ref, m_ref, h_ref, slot_ref, owner_ref, stars_ref, state_ref):
    x, v, a, j, m, h = (x_ref[...], v_ref[...], a_ref[...], j_ref[...], m_ref[...], h_ref[...])
    xp, vp = predict(x, v, a, j, h)
    members = x.shape[1]
    actives = slot_ref.shape[1]
    star = jnp.concatenate([xp, vp, m, jnp.zeros((1, members), jnp.float32)], axis=0)
    for k in range(stars_ref.shape[0]):
        stars_ref[k] = star
    team = lax.axis_index("team")
    wanted = jnp.where(owner_ref[...] == team, slot_ref[...], -1)
    chooser = (lax.broadcasted_iota(jnp.int32, (members, actives), 0) == wanted).astype(jnp.float32)
    state = jnp.concatenate([x, v, a, j, h, jnp.zeros((3, members), jnp.float32)], axis=0)
    chosen = jnp.dot(state, chooser, precision=lax.Precision.HIGHEST, preferred_element_type=jnp.float32)
    for k in range(state_ref.shape[0]):
        state_ref[k] = chosen


def force_kernel(stars_ref, state_ref, out_ref, row_ref, col_ref, acc_ref):
    n_gather, _, members = stars_ref.shape
    n_team = state_ref.shape[0] // out_blocks(state_ref)
    n_blocks = out_blocks(state_ref)
    halves = members // LANES
    n_rows = n_gather * halves

    def spread(r, _):
        block = stars_ref[r]
        for half in range(halves):
            for q in range(7):
                row_ref[q, r * halves + half] = jnp.broadcast_to(
                    block[q : q + 1, half * LANES : (half + 1) * LANES], (8, LANES)
                )
        return 0

    lax.fori_loop(0, n_gather, spread, 0)

    for b in range(n_blocks):
        state = state_ref[b]
        for t in range(1, n_team):
            state = state + state_ref[t * n_blocks + b]
        xi, vi = predict(state[0:3], state[3:6], state[6:9], state[9:12], state[12:13])
        pack = jnp.concatenate([xi, vi, jnp.zeros((2, LANES), jnp.float32)], axis=0)
        col_ref[pl.ds(b * LANES, LANES), :] = pack.T

    groups = 2

    def one_group(g, _):
        ivals = []
        for u in range(groups):
            cols = col_ref[pl.ds((g * groups + u) * 8, 8), :]
            ivals.append([jnp.broadcast_to(cols[:, q : q + 1], (8, LANES)) for q in range(6)])

        def one_row(r, acc):
            px, py, pz, ux, uy, uz, m = [row_ref[q, r] for q in range(7)]
            new = []
            for u in range(groups):
                xi, yi, zi, vxi, vyi, vzi = ivals[u]
                dx, dy, dz = px - xi, py - yi, pz - zi
                dvx, dvy, dvz = ux - vxi, uy - vyi, uz - vzi
                r2 = dx * dx + dy * dy + dz * dz + SOFTEN2
                inv = lax.rsqrt(r2)
                inv2 = inv * inv
                w = m * inv * inv2
                f = w * (inv2 * (dx * dvx + dy * dvy + dz * dvz))
                a = acc[u * 9 : u * 9 + 9]
                new += [
                    a[0] + w * dx, a[1] + w * dy, a[2] + w * dz,
                    a[3] + w * dvx, a[4] + w * dvy, a[5] + w * dvz,
                    a[6] + f * dx, a[7] + f * dy, a[8] + f * dz,
                ]
            return tuple(new)

        acc = lax.fori_loop(0, n_rows, one_row, tuple(jnp.zeros((8, LANES), jnp.float32) for _ in range(9 * groups)), unroll=2)
        for u in range(groups):
            a = acc[u * 9 : u * 9 + 9]
            at = pl.ds((g * groups + u) * 8, 8)
            for q in range(3):
                acc_ref[q, at, :] = a[q]
                acc_ref[3 + q, at, :] = a[3 + q] - 3.0 * a[6 + q]
        return 0

    lax.fori_loop(0, n_blocks * LANES // (8 * groups), one_group, 0)

    for b in range(n_blocks):
        rows = [jnp.sum(acc_ref[q, pl.ds(b * LANES, LANES), :].T, axis=0, keepdims=True) for q in range(6)]
        part = jnp.concatenate(rows + [jnp.zeros((2, LANES), jnp.float32)], axis=0)
        for t in range(n_team):
            out_ref[t * n_blocks + b] = part


def out_blocks(state_ref):
    return N_YLO * N_CORE


def correct_kernel(part_ref, state_ref, phase_ref, force_ref, higher_ref):
    n = part_ref.shape[0]
    n_blocks = N_YLO * N_CORE
    mine = lax.axis_index("y") * N_CORE + lax.axis_index("core")
    total = part_ref[0]
    for k in range(1, n):
        total = total + part_ref[k]
    own = state_ref[mine]
    for t in range(1, n // n_blocks):
        own = own + state_ref[t * n_blocks + mine]
    x0, v0, a0, j0, dt = (own[0:3], own[3:6], own[6:9], own[9:12], own[12:13])
    a1, j1 = (total[0:3], total[3:6])
    v1 = v0 + (a0 + a1) * dt / 2.0 + (j0 - j1) * dt * dt / 12.0
    x1 = x0 + (v0 + v1) * dt / 2.0 + (a0 - a1) * dt * dt / 12.0
    snap = -6.0 * (a0 - a1) - dt * (4.0 * j0 + 2.0 * j1)
    crackle = 12.0 * (a0 - a1) + 6.0 * dt * (j0 + j1)
    phase_ref[...] = jnp.concatenate([x1, v1], 0)
    force_ref[...] = total[0:6]
    higher_ref[...] = jnp.concatenate([snap, crackle], 0)


def shards(sizes, position, velocity, old_accel, old_jerk, mass, elapsed, active_slot, active_owner):
    members = position.shape[1]
    actives = active_slot.shape[0]
    n_gather = sizes["x"] * sizes["z"]
    n_reduce = sizes["team"] * sizes["y"] * sizes["core"]
    n_blocks = sizes["y"] * sizes["core"]
    f32 = jnp.float32
    stars, state = pl.pallas_call(
        pack_kernel,
        out_shape=(
            jax.ShapeDtypeStruct((n_gather, 8, members), f32),
            jax.ShapeDtypeStruct((n_reduce, 16, actives), f32),
        ),
        name="pack",
    )(
        position, velocity, old_accel, old_jerk, mass.reshape(1, members), elapsed.reshape(1, members),
        active_slot.reshape(1, actives), active_owner.reshape(1, actives),
    )
    state = lax.all_to_all(state, REDUCE, 0, 0, tiled=True)
    stars = lax.all_to_all(stars, GATHER, 0, 0, tiled=True)
    n_rows = n_gather * members // LANES
    part = pl.pallas_call(
        force_kernel,
        out_shape=jax.ShapeDtypeStruct((n_reduce, 8, actives), f32),
        scratch_shapes=[
            pltpu.VMEM((7, n_rows, 8, LANES), f32),
            pltpu.VMEM((n_blocks * actives, 8), f32),
            pltpu.VMEM((6, n_blocks * actives, LANES), f32),
        ],
        compiler_params=pltpu.CompilerParams(vmem_limit_bytes=32 * 1024 * 1024),
        name="force",
    )(stars, state)
    part = lax.all_to_all(part, REDUCE, 0, 0, tiled=True)
    out = jax.ShapeDtypeStruct((6, actives), f32)
    return pl.pallas_call(correct_kernel, out_shape=(out, out, out), name="correct")(part, state)


def solution(mesh):
    n_team = mesh.shape["team"]
    fine = Mesh(
        mesh.devices.reshape(n_team, N_X, N_YLO, N_Z, N_CORE), ("team", "x", "y", "z", "core")
    )
    blk = ("x", "y", "z", "core")
    whole = ("team",) + blk
    placed = (
        P(None, whole), P(None, whole), P(None, whole), P(None, whole),
        P(whole), P(whole), P(blk), P(blk),
    )
    return jax.shard_map(
        functools.partial(shards, dict(fine.shape)),
        mesh=fine,
        in_specs=placed,
        out_specs=(P(None, blk), P(None, blk), P(None, blk)),
        check_vma=False,
    )
```

time: 254 us -> 92.9 us (0.37)
  blocking collectives: 188 us -> 53.9 us
  other arithmetic: 45.9 us -> 0 us
  Pallas kernels: 0 us -> 38 us
  local copies, waits for them, and re-layouts: 16.6 us -> 0.01 us
  loops' own time: 2.64 us -> 0 us
    all_gather x1 -> x0, blocking collectives: 167 us -> none  [shards(): piece = lax.all_gather(jpack, 'blk', axis=1, tiled=True)]
    all_to_all x0 -> x3, blocking collectives: none -> 53.9 us  [the longest x1 21.8 us: shards(): stars = lax.all_to_all(stars, GATHER, 0, 0, tiled=True)]
    reduce_sum x128 -> x0, other arithmetic: 39.5 us -> none  [the longest x64 25.7 us: pair_block(): acc = jnp.sum(weight * dx, axis=2)]
    pallas_call x0 -> x3, Pallas kernels: none -> 38 us  [the longest x1 34.8 us: shards(): pl.pallas_call(force_kernel, out_shape=jax.ShapeDtypeStruct((n_reduce, 8,...]
    psum x2 -> x0, blocking collectives: 20.6 us -> none  [the longest x1 11.8 us: shards(): own = lax.psum(chosen, 'team')]
    slice x128 -> x0, local copies, waits for them, and re-layouts: 10.4 us -> none  [the longest x64 5.22 us: pair_block(): weight = jpack[6][None, :] * inv * inv * inv]
    div x64 -> x0, other arithmetic: 5.05 us -> none  [pair_block(): rv = 3.0 * jnp.sum(dx * dv, axis=0) / r2]
    unnamed x18 -> x4, local copies, waits for them, and re-layouts: 3.91 us -> 0.01 us
where the time goes in v1:
time: 92.9 us; the launch traced here: 92.6 us
  blocking collectives  53.9 us (58%)
  Pallas kernels  38 us (41%)
    pallas_call x1, Pallas kernels, shards(): pl.pallas_call(force_kernel, out_shape=jax.ShapeDtypeStruct((n_reduce, 8,...  34.8 us
    all_to_all x1, blocking collectives, shards(): stars = lax.all_to_all(stars, GATHER, 0, 0, tiled=True)  21.8 us
    all_to_all x1, blocking collectives, shards(): state = lax.all_to_all(state, REDUCE, 0, 0, tiled=True)  19.5 us
    all_to_all x1, blocking collectives, shards(): part = lax.all_to_all(part, REDUCE, 0, 0, tiled=True)  12.6 us

profile of v1, /device:TPU:1, one launch (start us, length us, event | category | flops | bytes accessed | tf_op | source)
XLA Modules:
  0.0 92.6 jit_solution(1471775977136645737)
XLA Ops:
  0.6 1.7 %pack.1 = (f32[32,8,256]{2,1,0:T(8,128)}, f32[16,16,128]{2,1,0:T(8,128)}) custom-call(f32[3,256]{1,0:T(4,128)} %x_ref.1, f32[3,256]{1,0:T(4,128)} %v_ref.1, f32[3,256]{1,0:T(4,128)} %a_ref.1, f32[3,256]{1,0:T(4,128)} %j_ref.1, f32[1,256]{1,0:T(1,128)} %bitcast.4, f32[1,256]{1,0:T(1,128)} %bitcast.5, s32[1,128]{1,0:T(1,128)} %bitcast.6, s32[1,128]{1,0:T(1,128)} %bitcast.7), custom_call_target="tpu_custom_call" | custom-call | tf_op jit(solution)/shard_map/pack/pallas_call | solution.py:143
  2.3 0.0 copy-start.1
  2.3 19.5 %all_to_all.15.state_ref = f32[16,16,128]{2,1,0:T(8,128)S(1)} all-to-all(f32[16,16,128]{2,1,0:T(8,128)} %get-tuple-element.6), channel_id=1, replica_groups=mesh['team'=4,'x'=4,'y'=2,'z'=8,'core'=2] {'team','y','core'}, dimensions={0} | all-to-all | bytes 262144 | tf_op jit(solution)/shard_map/all_to_all | solution.py:154
  21.8 0.0 copy-start
  21.8 0.0 copy-done.1
  21.8 21.8 %all_to_all.16.stars_ref = f32[32,8,256]{2,1,0:T(8,128)S(1)} all-to-all(f32[32,8,256]{2,1,0:T(8,128)S(1)} %copy-done.1), channel_id=1, replica_groups=mesh['team'=4,'x'=4,'y'=2,'z'=8,'core'=2] {'x','z'}, dimensions={0} | all-to-all | bytes 524288 | tf_op jit(solution)/shard_map/all_to_all | solution.py:155
  43.6 0.0 copy-done
  43.6 34.8 %force.1 = f32[16,8,128]{2,1,0:T(8,128)S(1)} custom-call(f32[32,8,256]{2,1,0:T(8,128)S(1)} %all_to_all.16.stars_ref, f32[16,16,128]{2,1,0:T(8,128)S(1)} %all_to_all.15.state_ref), custom_call_target="tpu_custom_call" | custom-call | tf_op jit(solution)/shard_map/force/pallas_call | solution.py:157
  78.4 12.6 %all_to_all.17.part_ref = f32[16,8,128]{2,1,0:T(8,128)} all-to-all(f32[16,8,128]{2,1,0:T(8,128)S(1)} %force.1), channel_id=1, replica_groups=mesh['team'=4,'x'=4,'y'=2,'z'=8,'core'=2] {'team','y','core'}, dimensions={0} | all-to-all | bytes 131072 | tf_op jit(solution)/shard_map/all_to_all | solution.py:168
  91.1 1.6 %correct.1 = (f32[6,128]{1,0:T(8,128)}, f32[6,128]{1,0:T(8,128)}, f32[6,128]{1,0:T(8,128)}) custom-call(f32[16,8,128]{2,1,0:T(8,128)} %all_to_all.17.part_ref, f32[16,16,128]{2,1,0:T(8,128)} %copy-done), custom_call_target="tpu_custom_call" | custom-call | tf_op jit(solution)/shard_map/correct/pallas_call | solution.py:170
Async XLA Ops:
  2.3 19.5 %copy-start.1 = (f32[32,8,256]{2,1,0:T(8,128)S(1)}, f32[32,8,256]{2,1,0:T(8,128)}, u32[]{:S(2)}) copy-start(f32[32,8,256]{2,1,0:T(8,128)} %get-tuple-element.5) | copy-start | bytes 786436
  21.8 21.8 %copy-start = (f32[16,16,128]{2,1,0:T(8,128)}, f32[16,16,128]{2,1,0:T(8,128)S(1)}, u32[]{:S(2)}) copy-start(f32[16,16,128]{2,1,0:T(8,128)S(1)} %all_to_all.15.state_ref) | copy-start | bytes 393220

commit v2 on v1

v2 whole, which is shorter than its diff:
```python
import functools
import jax
import jax.numpy as jnp
from jax import lax
from jax.experimental import pallas as pl
from jax.experimental.pallas import tpu as pltpu
from jax.sharding import Mesh, PartitionSpec as P

SOFTEN2 = 0.0001
N_X, N_YLO, N_Z, N_CORE = 4, 2, 8, 2
LANES = 128
GATHER = ("x", "z")
REDUCE = ("team", "y", "core")
CHUNK = 1024
N_MATRIX = 256
F32 = jnp.float32
BF16 = jnp.bfloat16


def predict(x, v, a, j, h):
    xp = x + h * (v + h * (a / 2.0 + h * j / 6.0))
    vp = v + h * (a + h * j / 2.0)
    return (xp, vp)


def pack_kernel(x_ref, v_ref, a_ref, j_ref, m_ref, h_ref, slot_ref, owner_ref, stars_ref, state_ref):
    x, v, a, j, m, h = (x_ref[...], v_ref[...], a_ref[...], j_ref[...], m_ref[...], h_ref[...])
    xp, vp = predict(x, v, a, j, h)
    members = x.shape[1]
    actives = slot_ref.shape[1]
    star = jnp.concatenate([xp, vp, m, jnp.zeros((1, members), jnp.float32)], axis=0)
    for k in range(stars_ref.shape[0]):
        stars_ref[k] = star
    team = lax.axis_index("team")
    wanted = jnp.where(owner_ref[...] == team, slot_ref[...], -1)
    chooser = (lax.broadcasted_iota(jnp.int32, (members, actives), 0) == wanted).astype(jnp.float32)
    state = jnp.concatenate([x, v, a, j, h, jnp.zeros((3, members), jnp.float32)], axis=0)
    chosen = jnp.dot(state, chooser, precision=lax.Precision.HIGHEST, preferred_element_type=jnp.float32)
    for k in range(state_ref.shape[0]):
        state_ref[k] = chosen


def pieces(value, count):
    out = []
    for _ in range(count - 1):
        piece = value.astype(BF16).astype(F32)
        out.append(piece)
        value = value - piece
    out.append(value.astype(BF16).astype(F32))
    return out


def grid_pieces(value):
    high = jnp.round(value * 64.0) * (1.0 / 64.0)
    first = high.astype(BF16).astype(F32)
    low = value - high
    third = low.astype(BF16).astype(F32)
    return high, low, [first, high - first, third, (low - third).astype(BF16).astype(F32)]


def sum3(rows):
    return rows[0:1] + rows[1:2] + rows[2:3]


def own_terms(high, low, value):
    coarse = sum3(high[0:3] * high[0:3])
    fine = sum3(low[0:3] * (2.0 * high[0:3] + low[0:3]))
    cross = sum3(value[0:3] * value[3:6])
    return pieces(coarse, 3), pieces(fine, 3), pieces(cross, 3)


def star_rows(block):
    n = block.shape[1]
    high, low, p = grid_pieces(block)
    coarse, fine, cross = own_terms(high, low, block)
    one, zero = jnp.ones((1, n), F32), jnp.zeros((1, n), F32)
    stack = []
    for k in range(3):
        stack += [jnp.concatenate([p[k][0:6], coarse[k], fine[k]], 0)] * 4
    stack += [jnp.concatenate([p[3][0:6], one, zero], 0)] * 3
    stack += [jnp.concatenate(cross + [block[0:3], zero, zero], 0)]
    return jnp.concatenate(stack, 0)


def active_rows(pack):
    n = pack.shape[1]
    high, low, p = grid_pieces(pack)
    coarse, fine, cross = own_terms(high, low, pack)
    fine = pieces(sum3(low[0:3] * (2.0 * high[0:3] + low[0:3])) + SOFTEN2, 3)
    zero3, zero, one = jnp.zeros((3, n), F32), jnp.zeros((1, n), F32), jnp.ones((1, n), F32)
    ra, rb, rc = [], [], []
    for k in range(4):
        for l in range(4 if k < 3 else 3):
            is_coarse = k < 2 and l < 2
            unit = one if (l == 0 and k < 3) else zero
            twice = -2.0 * p[l][0:3]
            last = k == 3
            ra.append(jnp.concatenate([twice if is_coarse else zero3, zero3, coarse[l] if last else unit, zero], 0))
            rb.append(jnp.concatenate([zero3 if is_coarse else twice, zero3, fine[l] if last else zero, unit], 0))
            rc.append(jnp.concatenate([-p[l][3:6], -p[l][0:3], cross[l] if last else zero, zero], 0))
    ra.append(jnp.zeros((8, n), F32))
    rb.append(jnp.zeros((8, n), F32))
    rc.append(jnp.concatenate([jnp.ones((3, n), F32), jnp.zeros((5, n), F32)], 0))
    return [jnp.concatenate(rows, 0) for rows in (ra, rb, rc)]


def force_kernel(stars_ref, state_ref, out_ref, met_ref, act_ref):
    n_gather, _, members = stars_ref.shape
    n_blocks = N_YLO * N_CORE
    n_team = state_ref.shape[0] // n_blocks
    n_act = n_blocks * LANES
    per = CHUNK // members
    nm = N_MATRIX
    for b in range(n_blocks):
        state = state_ref[b]
        for t in range(1, n_team):
            state = state + state_ref[t * n_blocks + b]
        xi, vi = predict(state[0:3], state[3:6], state[6:9], state[9:12], state[12:13])
        pack = jnp.concatenate([xi, vi, jnp.zeros((2, LANES), F32)], 0)
        at = b * LANES
        act_ref[:, at : at + LANES] = pack
        ra, rb, rc = active_rows(pack)
        if at < nm:
            met_ref[:, at : at + LANES] = ra.astype(BF16)
            met_ref[:, nm + at : nm + at + LANES] = rb.astype(BF16)
        met_ref[:, 2 * nm + at : 2 * nm + at + LANES] = rc.astype(BF16)

    def one_chunk(c, acc):
        cols, back = [], []
        for q in range(per):
            block = stars_ref[c * per + q]
            cols.append(star_rows(block).T)
            heavy = jnp.concatenate([block[0:6] * block[6:7], block[6:8]], 0)
            back.append(jnp.concatenate(pieces(heavy, 3), 0))
        cols = jnp.concatenate(cols, 0)
        back = jnp.concatenate(back, 1).astype(BF16)
        feats = cols.astype(BF16)
        two = jnp.dot(feats, met_ref[:, : 2 * nm], preferred_element_type=F32)
        cross = jnp.dot(feats, met_ref[:, 2 * nm :], preferred_element_type=F32)
        d = [cols[:, 123 + q : 124 + q] - act_ref[q : q + 1, nm:] for q in range(3)]
        r2 = jnp.concatenate(
            [two[:, :nm] + two[:, nm:], d[0] * d[0] + d[1] * d[1] + d[2] * d[2] + SOFTEN2], 1
        )
        inv = lax.rsqrt(r2)
        inv2 = inv * inv
        w = inv * inv2
        u = w * inv2 * cross
        sums = []
        for value in (w, u):
            upper = value.astype(BF16)
            lower = (value - upper.astype(F32)).astype(BF16)
            sums.append(
                jnp.dot(back, upper, preferred_element_type=F32)
                + jnp.dot(back, lower, preferred_element_type=F32)
            )
        return acc[0] + sums[0], acc[1] + sums[1]

    zero = jnp.zeros((24, n_act), F32)
    sw, su = lax.fori_loop(0, n_gather * members // CHUNK, one_chunk, (zero, zero), unroll=2)
    sw = sw[16:24] + sw[8:16] + sw[0:8]
    su = su[16:24] + su[8:16] + su[0:8]
    xi, vi = act_ref[0:3, :], act_ref[3:6, :]
    a = sw[0:3] - xi * sw[6:7]
    j = (sw[3:6] - vi * sw[6:7]) - 3.0 * (su[0:3] - xi * su[6:7])
    part = jnp.concatenate([a, j, jnp.zeros((2, n_act), F32)], 0)
    for b in range(n_blocks):
        for t in range(n_team):
            out_ref[t * n_blocks + b] = part[:, b * LANES : (b + 1) * LANES]


def correct_kernel(part_ref, state_ref, phase_ref, force_ref, higher_ref):
    n = part_ref.shape[0]
    n_blocks = N_YLO * N_CORE
    mine = lax.axis_index("y") * N_CORE + lax.axis_index("core")
    total = part_ref[0]
    for k in range(1, n):
        total = total + part_ref[k]
    own = state_ref[mine]
    for t in range(1, n // n_blocks):
        own = own + state_ref[t * n_blocks + mine]
    x0, v0, a0, j0, dt = (own[0:3], own[3:6], own[6:9], own[9:12], own[12:13])
    a1, j1 = (total[0:3], total[3:6])
    v1 = v0 + (a0 + a1) * dt / 2.0 + (j0 - j1) * dt * dt / 12.0
    x1 = x0 + (v0 + v1) * dt / 2.0 + (a0 - a1) * dt * dt / 12.0
    snap = -6.0 * (a0 - a1) - dt * (4.0 * j0 + 2.0 * j1)
    crackle = 12.0 * (a0 - a1) + 6.0 * dt * (j0 + j1)
    phase_ref[...] = jnp.concatenate([x1, v1], 0)
    force_ref[...] = total[0:6]
    higher_ref[...] = jnp.concatenate([snap, crackle], 0)


def shards(sizes, position, velocity, old_accel, old_jerk, mass, elapsed, active_slot, active_owner):
    members = position.shape[1]
    actives = active_slot.shape[0]
    n_gather = sizes["x"] * sizes["z"]
    n_reduce = sizes["team"] * sizes["y"] * sizes["core"]
    n_blocks = sizes["y"] * sizes["core"]
    stars, state = pl.pallas_call(
        pack_kernel,
        out_shape=(
            jax.ShapeDtypeStruct((n_gather, 8, members), F32),
            jax.ShapeDtypeStruct((n_reduce, 16, actives), F32),
        ),
        name="pack",
    )(
        position, velocity, old_accel, old_jerk, mass.reshape(1, members), elapsed.reshape(1, members),
        active_slot.reshape(1, actives), active_owner.reshape(1, actives),
    )
    state = lax.all_to_all(state, REDUCE, 0, 0, tiled=True)
    stars = lax.all_to_all(stars, GATHER, 0, 0, tiled=True)
    part = pl.pallas_call(
        force_kernel,
        out_shape=jax.ShapeDtypeStruct((n_reduce, 8, actives), F32),
        scratch_shapes=[
            pltpu.VMEM((LANES, 2 * N_MATRIX + n_blocks * actives), BF16),
            pltpu.VMEM((8, n_blocks * actives), F32),
        ],
        compiler_params=pltpu.CompilerParams(vmem_limit_bytes=48 * 1024 * 1024),
        name="force",
    )(stars, state)
    part = lax.all_to_all(part, REDUCE, 0, 0, tiled=True)
    out = jax.ShapeDtypeStruct((6, actives), F32)
    return pl.pallas_call(correct_kernel, out_shape=(out, out, out), name="correct")(part, state)


def solution(mesh):
    n_team = mesh.shape["team"]
    fine = Mesh(
        mesh.devices.reshape(n_team, N_X, N_YLO, N_Z, N_CORE), ("team", "x", "y", "z", "core")
    )
    blk = ("x", "y", "z", "core")
    whole = ("team",) + blk
    placed = (
        P(None, whole), P(None, whole), P(None, whole), P(None, whole),
        P(whole), P(whole), P(blk), P(blk),
    )
    return jax.shard_map(
        functools.partial(shards, dict(fine.shape)),
        mesh=fine,
        in_specs=placed,
        out_specs=(P(None, blk), P(None, blk), P(None, blk)),
        check_vma=False,
    )
```

time: 92.9 us -> 71.5 us (0.77)
  Pallas kernels: 38 us -> 16.6 us
    pallas_call x1, Pallas kernels: 34.8 us -> 13.4 us  [shards(): pl.pallas_call(force_kernel, out_shape=jax.ShapeDtypeStruct((n_reduce, 8,...]
where the time goes in v2:
time: 71.5 us; the launch traced here: 71.2 us
  blocking collectives  53.9 us (75%)
  Pallas kernels  16.6 us (23%)
    all_to_all x1, blocking collectives, shards(): stars = lax.all_to_all(stars, GATHER, 0, 0, tiled=True)  21.8 us
    all_to_all x1, blocking collectives, shards(): state = lax.all_to_all(state, REDUCE, 0, 0, tiled=True)  19.5 us
    pallas_call x1, Pallas kernels, shards(): pl.pallas_call(force_kernel, out_shape=jax.ShapeDtypeStruct((n_reduce, 8,...  13.4 us
    all_to_all x1, blocking collectives, shards(): part = lax.all_to_all(part, REDUCE, 0, 0, tiled=True)  12.6 us
    pallas_call x1, Pallas kernels, shards(): pl.pallas_call(pack_kernel, out_shape=(jax.ShapeDtypeStruct((n_gather, 8,...  1.65 us
    pallas_call x1, Pallas kernels, shards(): pl.pallas_call(correct_kernel, out_shape=(out, out, out), name='correct')  1.57 us

profile of v2, /device:TPU:1, one launch (start us, length us, event | category | flops | bytes accessed | tf_op | source)
XLA Modules:
  0.0 71.2 jit_solution(167750784602616968)
XLA Ops:
  0.6 1.7 %pack.1 = (f32[32,8,256]{2,1,0:T(8,128)}, f32[16,16,128]{2,1,0:T(8,128)}) custom-call(f32[3,256]{1,0:T(4,128)} %x_ref.1, f32[3,256]{1,0:T(4,128)} %v_ref.1, f32[3,256]{1,0:T(4,128)} %a_ref.1, f32[3,256]{1,0:T(4,128)} %j_ref.1, f32[1,256]{1,0:T(1,128)} %bitcast.4, f32[1,256]{1,0:T(1,128)} %bitcast.5, s32[1,128]{1,0:T(1,128)} %bitcast.6, s32[1,128]{1,0:T(1,128)} %bitcast.7), custom_call_target="tpu_custom_call" | custom-call | tf_op jit(solution)/shard_map/pack/pallas_call | solution.py:198
  2.3 0.0 copy-start.1
  2.3 19.5 %all_to_all.15.state_ref = f32[16,16,128]{2,1,0:T(8,128)S(1)} all-to-all(f32[16,16,128]{2,1,0:T(8,128)} %get-tuple-element.6), channel_id=1, replica_groups=mesh['team'=4,'x'=4,'y'=2,'z'=8,'core'=2] {'team','y','core'}, dimensions={0} | all-to-all | bytes 262144 | tf_op jit(solution)/shard_map/all_to_all | solution.py:209
  21.8 0.0 copy-start
  21.8 0.0 copy-done.1
  21.8 21.8 %all_to_all.16.stars_ref = f32[32,8,256]{2,1,0:T(8,128)S(1)} all-to-all(f32[32,8,256]{2,1,0:T(8,128)S(1)} %copy-done.1), channel_id=1, replica_groups=mesh['team'=4,'x'=4,'y'=2,'z'=8,'core'=2] {'x','z'}, dimensions={0} | all-to-all | bytes 524288 | tf_op jit(solution)/shard_map/all_to_all | solution.py:210
  43.6 0.0 copy-done
  43.6 13.4 %force.1 = f32[16,8,128]{2,1,0:T(8,128)S(1)} custom-call(f32[32,8,256]{2,1,0:T(8,128)S(1)} %all_to_all.16.stars_ref, f32[16,16,128]{2,1,0:T(8,128)S(1)} %all_to_all.15.state_ref), custom_call_target="tpu_custom_call" | custom-call | tf_op jit(solution)/shard_map/force/pallas_call | solution.py:211
  57.0 12.6 %all_to_all.17.part_ref = f32[16,8,128]{2,1,0:T(8,128)} all-to-all(f32[16,8,128]{2,1,0:T(8,128)S(1)} %force.1), channel_id=1, replica_groups=mesh['team'=4,'x'=4,'y'=2,'z'=8,'core'=2] {'team','y','core'}, dimensions={0} | all-to-all | bytes 131072 | tf_op jit(solution)/shard_map/all_to_all | solution.py:221
  69.6 1.6 %correct.1 = (f32[6,128]{1,0:T(8,128)}, f32[6,128]{1,0:T(8,128)}, f32[6,128]{1,0:T(8,128)}) custom-call(f32[16,8,128]{2,1,0:T(8,128)} %all_to_all.17.part_ref, f32[16,16,128]{2,1,0:T(8,128)} %copy-done), custom_call_target="tpu_custom_call" | custom-call | tf_op jit(solution)/shard_map/correct/pallas_call | solution.py:223
Async XLA Ops:
  2.3 19.5 %copy-start.1 = (f32[32,8,256]{2,1,0:T(8,128)S(1)}, f32[32,8,256]{2,1,0:T(8,128)}, u32[]{:S(2)}) copy-start(f32[32,8,256]{2,1,0:T(8,128)} %get-tuple-element.5) | copy-start | bytes 786436
  21.8 21.8 %copy-start = (f32[16,16,128]{2,1,0:T(8,128)}, f32[16,16,128]{2,1,0:T(8,128)S(1)}, u32[]{:S(2)}) copy-start(f32[16,16,128]{2,1,0:T(8,128)S(1)} %all_to_all.15.state_ref) | copy-start | bytes 393220

commit v3 on v2

--- a/solution.py
+++ b/solution.py
@@ -11,8 +11,8 @@
 LANES = 128
 GATHER = ("x", "z")
 REDUCE = ("team", "y", "core")
-CHUNK = 1024
-N_MATRIX = 256
+SIDE = 256
+CYCLE = 4
 F32 = jnp.float32
 BF16 = jnp.bfloat16
 
@@ -40,53 +40,61 @@
         state_ref[k] = chosen
 
 
-def pieces(value, count):
-    out = []
-    for _ in range(count - 1):
-        piece = value.astype(BF16).astype(F32)
-        out.append(piece)
-        value = value - piece
-    out.append(value.astype(BF16).astype(F32))
-    return out
+def rounded(value):
+    return value.astype(BF16).astype(F32)
+
+
+def pieces(value):
+    first = rounded(value)
+    rest = value - first
+    second = rounded(rest)
+    return [first, second, rest - second]
 
 
 def grid_pieces(value):
-    high = jnp.round(value * 64.0) * (1.0 / 64.0)
-    first = high.astype(BF16).astype(F32)
+    high = jnp.round(value * 128.0) * (1.0 / 128.0)
+    first = rounded(high)
     low = value - high
-    third = low.astype(BF16).astype(F32)
-    return high, low, [first, high - first, third, (low - third).astype(BF16).astype(F32)]
+    third = rounded(low)
+    return high, low, [first, high - first, third, low - third]
+
+
+def star_rows(block):
+    row = lax.broadcasted_iota(jnp.int32, block.shape, 0)
+
+    def roll(value, shift):
+        return pltpu.roll(value, shift, 0)
+
+    moving = jnp.where(row < 6, block, 0.0)
+    high, low, p = grid_pieces(moving)
+    square = high * high
+    twice = low * (2.0 * high + low)
+    coarse = roll(square, 6) + roll(square, 5) + roll(square, 4)
+    fine = roll(twice, 7) + roll(twice, 6) + roll(twice, 5)
+    own = pieces(jnp.where(row == 6, coarse, jnp.where(row == 7, fine, 0.0)))
+    both = moving * roll(moving, 5)
+    cross = both + roll(both, 7) + roll(both, 6)
+    c = pieces(jnp.broadcast_to(cross[0:1], cross.shape))
+    last = jnp.where(row < 6, roll(block, 3), 0.0)
+    for k in range(3):
+        last = jnp.where(row == k, c[k], last)
+    stack = []
+    for k in range(3):
+        stack += [p[k] + own[k]] * 4
+    stack += [jnp.where(row == 6, 1.0, p[3])] * 3 + [last]
+    return jnp.concatenate(stack, 0)
 
 
 def sum3(rows):
     return rows[0:1] + rows[1:2] + rows[2:3]
-
-
-def own_terms(high, low, value):
-    coarse = sum3(high[0:3] * high[0:3])
-    fine = sum3(low[0:3] * (2.0 * high[0:3] + low[0:3]))
-    cross = sum3(value[0:3] * value[3:6])
-    return pieces(coarse, 3), pieces(fine, 3), pieces(cross, 3)
-
-
-def star_rows(block):
-    n = block.shape[1]
-    high, low, p = grid_pieces(block)
-    coarse, fine, cross = own_terms(high, low, block)
-    one, zero = jnp.ones((1, n), F32), jnp.zeros((1, n), F32)
-    stack = []
-    for k in range(3):
-        stack += [jnp.concatenate([p[k][0:6], coarse[k], fine[k]], 0)] * 4
-    stack += [jnp.concatenate([p[3][0:6], one, zero], 0)] * 3
-    stack += [jnp.concatenate(cross + [block[0:3], zero, zero], 0)]
-    return jnp.concatenate(stack, 0)
 
 
 def active_rows(pack):
     n = pack.shape[1]
     high, low, p = grid_pieces(pack)
-    coarse, fine, cross = own_terms(high, low, pack)
-    fine = pieces(sum3(low[0:3] * (2.0 * high[0:3] + low[0:3])) + SOFTEN2, 3)
+    coarse = pieces(sum3(high[0:3] * high[0:3]))
+    fine = pieces(sum3(low[0:3] * (2.0 * high[0:3] + low[0:3])) + SOFTEN2)
+    cross = pieces(sum3(pack[0:3] * pack[3:6]))
     zero3, zero, one = jnp.zeros((3, n), F32), jnp.zeros((1, n), F32), jnp.ones((1, n), F32)
     ra, rb, rc = [], [], []
     for k in range(4):
@@ -104,13 +112,19 @@
     return [jnp.concatenate(rows, 0) for rows in (ra, rb, rc)]
 
 
-def force_kernel(stars_ref, state_ref, out_ref, met_ref, act_ref):
-    n_gather, _, members = stars_ref.shape
+def heavy_rows(block):
+    row = lax.broadcasted_iota(jnp.int32, block.shape, 0)
+    heavy = jnp.where(row == 6, block, block * block[6:7])
+    return jnp.concatenate(pieces(heavy), 0).astype(BF16)
+
+
+def force_kernel(stars_ref, state_ref, out_ref, met_ref, act_ref, sum_ref, feat_ref, prod_ref, weight_ref, col_ref):
+    n_tiles = stars_ref.shape[0]
     n_blocks = N_YLO * N_CORE
     n_team = state_ref.shape[0] // n_blocks
     n_act = n_blocks * LANES
-    per = CHUNK // members
-    nm = N_MATRIX
+    sides = range(0, n_act, SIDE)
+
     for b in range(n_blocks):
         state = state_ref[b]
         for t in range(1, n_team):
@@ -119,46 +133,74 @@
         pack = jnp.concatenate([xi, vi, jnp.zeros((2, LANES), F32)], 0)
         at = b * LANES
         act_ref[:, at : at + LANES] = pack
-        ra, rb, rc = active_rows(pack)
-        if at < nm:
-            met_ref[:, at : at + LANES] = ra.astype(BF16)
-            met_ref[:, nm + at : nm + at + LANES] = rb.astype(BF16)
-        met_ref[:, 2 * nm + at : 2 * nm + at + LANES] = rc.astype(BF16)
-
-    def one_chunk(c, acc):
-        cols, back = [], []
-        for q in range(per):
-            block = stars_ref[c * per + q]
-            cols.append(star_rows(block).T)
-            heavy = jnp.concatenate([block[0:6] * block[6:7], block[6:8]], 0)
-            back.append(jnp.concatenate(pieces(heavy, 3), 0))
-        cols = jnp.concatenate(cols, 0)
-        back = jnp.concatenate(back, 1).astype(BF16)
-        feats = cols.astype(BF16)
-        two = jnp.dot(feats, met_ref[:, : 2 * nm], preferred_element_type=F32)
-        cross = jnp.dot(feats, met_ref[:, 2 * nm :], preferred_element_type=F32)
-        d = [cols[:, 123 + q : 124 + q] - act_ref[q : q + 1, nm:] for q in range(3)]
-        r2 = jnp.concatenate(
-            [two[:, :nm] + two[:, nm:], d[0] * d[0] + d[1] * d[1] + d[2] * d[2] + SOFTEN2], 1
-        )
+        for k, rows in enumerate(active_rows(pack)):
+            met_ref[:, k * n_act + at : k * n_act + at + LANES] = rows.astype(BF16)
+
+    def on_matrix(tile, side):
+        return side < n_act // 2 or tile % CYCLE != CYCLE - 1
+
+    def prepare(t, tile):
+        cols = star_rows(stars_ref[t]).T
+        feat_ref[...] = cols.astype(BF16)
+        if not on_matrix(tile, n_act - 1):
+            col_ref[...] = cols
+
+    def products(side, tile):
+        for k in (0, 1, 2) if on_matrix(tile, side) else (2,):
+            at = k * n_act + side
+            prod_ref[:, at : at + SIDE] = jnp.dot(
+                feat_ref[...], met_ref[:, at : at + SIDE], preferred_element_type=F32
+            )
+
+    def weights(side, tile):
+        cross = prod_ref[:, 2 * n_act + side : 2 * n_act + side + SIDE]
+        if on_matrix(tile, side):
+            r2 = prod_ref[:, side : side + SIDE] + prod_ref[:, n_act + side : n_act + side + SIDE]
+        else:
+            cols = col_ref[...]
+            d = [cols[:, 123 + q : 124 + q] - act_ref[q : q + 1, side : side + SIDE] for q in range(3)]
+            r2 = d[0] * d[0] + d[1] * d[1] + d[2] * d[2] + SOFTEN2
         inv = lax.rsqrt(r2)
         inv2 = inv * inv
         w = inv * inv2
         u = w * inv2 * cross
-        sums = []
-        for value in (w, u):
+        for k, value in enumerate((w, u)):
             upper = value.astype(BF16)
-            lower = (value - upper.astype(F32)).astype(BF16)
-            sums.append(
-                jnp.dot(back, upper, preferred_element_type=F32)
-                + jnp.dot(back, lower, preferred_element_type=F32)
+            at = 2 * k * n_act + side
+            weight_ref[:, at : at + SIDE] = upper
+            at = at + n_act
+            weight_ref[:, at : at + SIDE] = (value - upper.astype(F32)).astype(BF16)
+
+    def add_up(heavy, side):
+        for k in range(2):
+            at = 2 * k * n_act + side
+            upper, lower = weight_ref[:, at : at + SIDE], weight_ref[:, at + n_act : at + n_act + SIDE]
+            part = jnp.dot(heavy, upper, preferred_element_type=F32) + jnp.dot(
+                heavy, lower, preferred_element_type=F32
             )
-        return acc[0] + sums[0], acc[1] + sums[1]
-
-    zero = jnp.zeros((24, n_act), F32)
-    sw, su = lax.fori_loop(0, n_gather * members // CHUNK, one_chunk, (zero, zero), unroll=2)
-    sw = sw[16:24] + sw[8:16] + sw[0:8]
-    su = su[16:24] + su[8:16] + su[0:8]
+            at = k * n_act + side
+            sum_ref[:, at : at + SIDE] = sum_ref[:, at : at + SIDE] + part
+
+    sum_ref[...] = jnp.zeros_like(sum_ref)
+    prepare(0, 0)
+    for side in sides:
+        products(side, 0)
+    prepare(1, 1)
+
+    def one_cycle(c, _):
+        for tile in range(CYCLE):
+            t = c * CYCLE + tile
+            heavy = heavy_rows(stars_ref[t])
+            for side in sides:
+                weights(side, tile)
+                products(side, tile + 1)
+                add_up(heavy, side)
+            prepare(jnp.minimum(t + 2, n_tiles - 1), tile + 2)
+        return 0
+
+    lax.fori_loop(0, n_tiles // CYCLE, one_cycle, 0, unroll=2)
+    sums = sum_ref[16:24, :] + sum_ref[8:16, :] + sum_ref[0:8, :]
+    sw, su = sums[:, :n_act], sums[:, n_act:]
     xi, vi = act_ref[0:3, :], act_ref[3:6, :]
     a = sw[0:3] - xi * sw[6:7]
     j = (sw[3:6] - vi * sw[6:7]) - 3.0 * (su[0:3] - xi * su[6:7])
@@ -208,12 +250,18 @@
     )
     state = lax.all_to_all(state, REDUCE, 0, 0, tiled=True)
     stars = lax.all_to_all(stars, GATHER, 0, 0, tiled=True)
+    n_act = n_blocks * actives
     part = pl.pallas_call(
         force_kernel,
         out_shape=jax.ShapeDtypeStruct((n_reduce, 8, actives), F32),
         scratch_shapes=[
-            pltpu.VMEM((LANES, 2 * N_MATRIX + n_blocks * actives), BF16),
-            pltpu.VMEM((8, n_blocks * actives), F32),
+            pltpu.VMEM((LANES, 3 * n_act), BF16),
+            pltpu.VMEM((8, n_act), F32),
+            pltpu.VMEM((24, 2 * n_act), F32),
+            pltpu.VMEM((members, LANES), BF16),
+            pltpu.VMEM((members, 3 * n_act), F32),
+            pltpu.VMEM((members, 4 * n_act), BF16),
+            pltpu.VMEM((members, LANES), F32),
         ],
         compiler_params=pltpu.CompilerParams(vmem_limit_bytes=48 * 1024 * 1024),
         name="force",

time: 71.5 us -> 69.5 us (0.972)
  Pallas kernels: 16.6 us -> 14.6 us
    pallas_call x1, Pallas kernels: 13.4 us -> 11.4 us  [shards(): pl.pallas_call(force_kernel, out_shape=jax.ShapeDtypeStruct((n_reduce, 8,...]
where the time goes in v3:
time: 69.5 us; the launch traced here: 69.2 us
  blocking collectives  53.9 us (78%)
  Pallas kernels  14.6 us (21%)
    all_to_all x1, blocking collectives, shards(): stars = lax.all_to_all(stars, GATHER, 0, 0, tiled=True)  21.8 us
    all_to_all x1, blocking collectives, shards(): state = lax.all_to_all(state, REDUCE, 0, 0, tiled=True)  19.5 us
    all_to_all x1, blocking collectives, shards(): part = lax.all_to_all(part, REDUCE, 0, 0, tiled=True)  12.6 us
    pallas_call x1, Pallas kernels, shards(): pl.pallas_call(force_kernel, out_shape=jax.ShapeDtypeStruct((n_reduce, 8,...  11.4 us
    pallas_call x1, Pallas kernels, shards(): pl.pallas_call(pack_kernel, out_shape=(jax.ShapeDtypeStruct((n_gather, 8,...  1.65 us
    pallas_call x1, Pallas kernels, shards(): pl.pallas_call(correct_kernel, out_shape=(out, out, out), name='correct')  1.57 us

profile of v3, /device:TPU:1, one launch (start us, length us, event | category | flops | bytes accessed | tf_op | source)
XLA Modules:
  0.0 69.2 jit_solution(11578824528823108056)
XLA Ops:
  0.6 1.7 %pack.1 = (f32[32,8,256]{2,1,0:T(8,128)}, f32[16,16,128]{2,1,0:T(8,128)}) custom-call(f32[3,256]{1,0:T(4,128)} %x_ref.1, f32[3,256]{1,0:T(4,128)} %v_ref.1, f32[3,256]{1,0:T(4,128)} %a_ref.1, f32[3,256]{1,0:T(4,128)} %j_ref.1, f32[1,256]{1,0:T(1,128)} %bitcast.4, f32[1,256]{1,0:T(1,128)} %bitcast.5, s32[1,128]{1,0:T(1,128)} %bitcast.6, s32[1,128]{1,0:T(1,128)} %bitcast.7), custom_call_target="tpu_custom_call" | custom-call | tf_op jit(solution)/shard_map/pack/pallas_call | solution.py:240
  2.3 0.0 copy-start.1
  2.3 19.5 %all_to_all.15.state_ref = f32[16,16,128]{2,1,0:T(8,128)S(1)} all-to-all(f32[16,16,128]{2,1,0:T(8,128)} %get-tuple-element.6), channel_id=1, replica_groups=mesh['team'=4,'x'=4,'y'=2,'z'=8,'core'=2] {'team','y','core'}, dimensions={0} | all-to-all | bytes 262144 | tf_op jit(solution)/shard_map/all_to_all | solution.py:251
  21.8 0.0 copy-start
  21.8 0.0 copy-done.1
  21.8 21.8 %all_to_all.16.stars_ref = f32[32,8,256]{2,1,0:T(8,128)S(1)} all-to-all(f32[32,8,256]{2,1,0:T(8,128)S(1)} %copy-done.1), channel_id=1, replica_groups=mesh['team'=4,'x'=4,'y'=2,'z'=8,'core'=2] {'x','z'}, dimensions={0} | all-to-all | bytes 524288 | tf_op jit(solution)/shard_map/all_to_all | solution.py:252
  43.6 0.0 copy-done
  43.6 11.4 %force.1 = f32[16,8,128]{2,1,0:T(8,128)S(1)} custom-call(f32[32,8,256]{2,1,0:T(8,128)S(1)} %all_to_all.16.stars_ref, f32[16,16,128]{2,1,0:T(8,128)S(1)} %all_to_all.15.state_ref), custom_call_target="tpu_custom_call" | custom-call | tf_op jit(solution)/shard_map/force/pallas_call | solution.py:254
  55.0 12.6 %all_to_all.17.part_ref = f32[16,8,128]{2,1,0:T(8,128)} all-to-all(f32[16,8,128]{2,1,0:T(8,128)S(1)} %force.1), channel_id=1, replica_groups=mesh['team'=4,'x'=4,'y'=2,'z'=8,'core'=2] {'team','y','core'}, dimensions={0} | all-to-all | bytes 131072 | tf_op jit(solution)/shard_map/all_to_all | solution.py:269
  67.7 1.6 %correct.1 = (f32[6,128]{1,0:T(8,128)}, f32[6,128]{1,0:T(8,128)}, f32[6,128]{1,0:T(8,128)}) custom-call(f32[16,8,128]{2,1,0:T(8,128)} %all_to_all.17.part_ref, f32[16,16,128]{2,1,0:T(8,128)} %copy-done), custom_call_target="tpu_custom_call" | custom-call | tf_op jit(solution)/shard_map/correct/pallas_call | solution.py:271
Async XLA Ops:
  2.3 19.5 %copy-start.1 = (f32[32,8,256]{2,1,0:T(8,128)S(1)}, f32[32,8,256]{2,1,0:T(8,128)}, u32[]{:S(2)}) copy-start(f32[32,8,256]{2,1,0:T(8,128)} %get-tuple-element.5) | copy-start | bytes 786436
  21.8 21.8 %copy-start = (f32[16,16,128]{2,1,0:T(8,128)}, f32[16,16,128]{2,1,0:T(8,128)S(1)}, u32[]{:S(2)}) copy-start(f32[16,16,128]{2,1,0:T(8,128)S(1)} %all_to_all.15.state_ref) | copy-start | bytes 393220

commit v4 on v3

--- a/solution.py
+++ b/solution.py
@@ -23,21 +23,25 @@
     return (xp, vp)
 
 
-def pack_kernel(x_ref, v_ref, a_ref, j_ref, m_ref, h_ref, slot_ref, owner_ref, stars_ref, state_ref):
-    x, v, a, j, m, h = (x_ref[...], v_ref[...], a_ref[...], j_ref[...], m_ref[...], h_ref[...])
-    xp, vp = predict(x, v, a, j, h)
-    members = x.shape[1]
-    actives = slot_ref.shape[1]
-    star = jnp.concatenate([xp, vp, m, jnp.zeros((1, members), jnp.float32)], axis=0)
+def state_kernel(x_ref, v_ref, a_ref, j_ref, h_ref, slot_ref, owner_ref, state_ref):
+    members, actives = x_ref.shape[1], slot_ref.shape[1]
+    team = lax.axis_index("team")
+    wanted = jnp.where(owner_ref[...] == team, slot_ref[...], -1)
+    chooser = (lax.broadcasted_iota(jnp.int32, (members, actives), 0) == wanted).astype(F32)
+    state = jnp.concatenate(
+        [x_ref[...], v_ref[...], a_ref[...], j_ref[...], h_ref[...], jnp.zeros((3, members), F32)], axis=0
+    )
+    chosen = jnp.dot(state, chooser, precision=lax.Precision.HIGHEST, preferred_element_type=F32)
+    for k in range(state_ref.shape[0]):
+        state_ref[k] = chosen
+
+
+def star_kernel(x_ref, v_ref, a_ref, j_ref, m_ref, h_ref, stars_ref):
+    xp, vp = predict(x_ref[...], v_ref[...], a_ref[...], j_ref[...], h_ref[...])
+    rows = [value[q : q + 1] for value in (xp, vp) for q in range(3)] + [m_ref[...]]
+    star = jnp.concatenate(rows, axis=1)
     for k in range(stars_ref.shape[0]):
         stars_ref[k] = star
-    team = lax.axis_index("team")
-    wanted = jnp.where(owner_ref[...] == team, slot_ref[...], -1)
-    chooser = (lax.broadcasted_iota(jnp.int32, (members, actives), 0) == wanted).astype(jnp.float32)
-    state = jnp.concatenate([x, v, a, j, h, jnp.zeros((3, members), jnp.float32)], axis=0)
-    chosen = jnp.dot(state, chooser, precision=lax.Precision.HIGHEST, preferred_element_type=jnp.float32)
-    for k in range(state_ref.shape[0]):
-        state_ref[k] = chosen
 
 
 def rounded(value):
@@ -136,11 +140,17 @@
         for k, rows in enumerate(active_rows(pack)):
             met_ref[:, k * n_act + at : k * n_act + at + LANES] = rows.astype(BF16)
 
+    def block_of(t):
+        line = stars_ref[t]
+        members = line.shape[1] // 7
+        rows = [line[:, q * members : (q + 1) * members] for q in range(7)]
+        return jnp.concatenate(rows + [jnp.zeros((1, members), F32)], 0)
+
     def on_matrix(tile, side):
         return side < n_act // 2 or tile % CYCLE != CYCLE - 1
 
     def prepare(t, tile):
-        cols = star_rows(stars_ref[t]).T
+        cols = star_rows(block_of(t)).T
         feat_ref[...] = cols.astype(BF16)
         if not on_matrix(tile, n_act - 1):
             col_ref[...] = cols
@@ -190,7 +200,7 @@
     def one_cycle(c, _):
         for tile in range(CYCLE):
             t = c * CYCLE + tile
-            heavy = heavy_rows(stars_ref[t])
+            heavy = heavy_rows(block_of(t))
             for side in sides:
                 weights(side, tile)
                 products(side, tile + 1)
@@ -237,17 +247,16 @@
     n_gather = sizes["x"] * sizes["z"]
     n_reduce = sizes["team"] * sizes["y"] * sizes["core"]
     n_blocks = sizes["y"] * sizes["core"]
-    stars, state = pl.pallas_call(
-        pack_kernel,
-        out_shape=(
-            jax.ShapeDtypeStruct((n_gather, 8, members), F32),
-            jax.ShapeDtypeStruct((n_reduce, 16, actives), F32),
-        ),
-        name="pack",
+    elapsed = elapsed.reshape(1, members)
+    state = pl.pallas_call(
+        state_kernel, out_shape=jax.ShapeDtypeStruct((n_reduce, 16, actives), F32), name="state"
     )(
-        position, velocity, old_accel, old_jerk, mass.reshape(1, members), elapsed.reshape(1, members),
+        position, velocity, old_accel, old_jerk, elapsed,
         active_slot.reshape(1, actives), active_owner.reshape(1, actives),
     )
+    stars = pl.pallas_call(
+        star_kernel, out_shape=jax.ShapeDtypeStruct((n_gather, 1, 7 * members), F32), name="stars"
+    )(position, velocity, old_accel, old_jerk, mass.reshape(1, members), elapsed)
     state = lax.all_to_all(state, REDUCE, 0, 0, tiled=True)
     stars = lax.all_to_all(stars, GATHER, 0, 0, tiled=True)
     n_act = n_blocks * actives

time: 69.5 us -> 69.3 us (level)
  blocking collectives: 53.9 us -> 34.1 us
  starting transfers between devices: 0 us -> 10.2 us
  waiting for transfers between devices: 0 us -> 7.73 us
  Pallas kernels: 14.6 us -> 16.2 us
    all_to_all x1 -> x0, blocking collectives: 19.5 us -> none  [shards(): state = lax.all_to_all(state, REDUCE, 0, 0, tiled=True)]
    all_to_all x0 -> x1, starting transfers between devices: none -> 10.2 us  [shards(): state = lax.all_to_all(state, REDUCE, 0, 0, tiled=True)]
    all_to_all x0 -> x1, waiting for transfers between devices: none -> 7.73 us  [shards(): state = lax.all_to_all(state, REDUCE, 0, 0, tiled=True)]
    pallas_call x1 -> x2, Pallas kernels: 1.65 us -> 3.1 us  [the longest x1 1.62 us: shards(): pl.pallas_call(state_kernel, out_shape=jax.ShapeDtypeStruct((n_reduce, 16...]
  transfers between devices with their start and end apart: 0 -> 1, of which waited for: 0 -> 1; matrix products, arithmetic and copies ran while one was open for 0% -> 0% of each run, Pallas kernels for 0% -> 2%
where the time goes in v4:
time: 69.3 us; the launch traced here: 68.9 us
  blocking collectives  34.1 us (49%)
  Pallas kernels  16.2 us (23%)
  starting transfers between devices  10.2 us (15%)
  waiting for transfers between devices  7.73 us (11%)
    all_to_all x1, blocking collectives, shards(): stars = lax.all_to_all(stars, GATHER, 0, 0, tiled=True)  21.6 us
    all_to_all x1, blocking collectives, shards(): part = lax.all_to_all(part, REDUCE, 0, 0, tiled=True)  12.5 us
    pallas_call x1, Pallas kernels, shards(): pl.pallas_call(force_kernel, out_shape=jax.ShapeDtypeStruct((n_reduce, 8,...  11.6 us
    all_to_all x1, starting transfers between devices, shards(): state = lax.all_to_all(state, REDUCE, 0, 0, tiled=True)  10.2 us
    all_to_all x1, waiting for transfers between devices, shards(): state = lax.all_to_all(state, REDUCE, 0, 0, tiled=True)  7.73 us
    pallas_call x1, Pallas kernels, shards(): pl.pallas_call(state_kernel, out_shape=jax.ShapeDtypeStruct((n_reduce, 16...  1.62 us
    pallas_call x1, Pallas kernels, shards(): pl.pallas_call(correct_kernel, out_shape=(out, out, out), name='correct')  1.57 us
    pallas_call x1, Pallas kernels, shards(): pl.pallas_call(star_kernel, out_shape=jax.ShapeDtypeStruct((n_gather, 1,...  1.48 us
  transfers between devices with their start and end apart: 1, of which 1 were waited for; matrix products, arithmetic and copies ran while one was open for 0% of the time, Pallas kernels for 2%

profile of v4, /device:TPU:1, one launch (start us, length us, event | category | flops | bytes accessed | tf_op | source)
XLA Modules:
  0.0 68.9 jit_solution(5169416277312554107)
XLA Ops:
  0.6 1.6 %state.1 = f32[16,16,128]{2,1,0:T(8,128)} custom-call(f32[3,256]{1,0:T(4,128)} %x_ref.3, f32[3,256]{1,0:T(4,128)} %v_ref.3, f32[3,256]{1,0:T(4,128)} %a_ref.3, f32[3,256]{1,0:T(4,128)} %j_ref.3, f32[1,256]{1,0:T(1,128)} %bitcast.4, s32[1,128]{1,0:T(1,128)} %bitcast.7, s32[1,128]{1,0:T(1,128)} %bitcast.8), custom_call_target="tpu_custom_call" | custom-call | tf_op jit(solution)/shard_map/state/pallas_call | solution.py:251
  2.3 10.2 %all-to-all-start.1 = ((f32[16,16,128]{2,1,0:T(8,128)}), f32[16,16,128]{2,1,0:T(8,128)S(1)}, u32[]{:S(2)}, u32[]{:S(2)}) async-start(f32[16,16,128]{2,1,0:T(8,128)} %state.1), calls=%async_computation.1 | async-start | bytes 262144 | tf_op jit(solution)/shard_map/all_to_all | solution.py:260
  12.4 1.5 %stars.1 = f32[32,1,1792]{2,1,0:T(1,128)} custom-call(f32[3,256]{1,0:T(4,128)} %x_ref.3, f32[3,256]{1,0:T(4,128)} %v_ref.3, f32[3,256]{1,0:T(4,128)} %a_ref.3, f32[3,256]{1,0:T(4,128)} %j_ref.3, f32[1,256]{1,0:T(1,128)} %bitcast.6, f32[1,256]{1,0:T(1,128)} %bitcast.5), custom_call_target="tpu_custom_call" | custom-call | tf_op jit(solution)/shard_map/stars/pallas_call | solution.py:257
  13.9 7.7 %all-to-all-done.1.state_ref = f32[16,16,128]{2,1,0:T(8,128)S(1)} async-done(((f32[16,16,128]{2,1,0:T(8,128)}), f32[16,16,128]{2,1,0:T(8,128)S(1)}, u32[]{:S(2)}, u32[]{:S(2)}) %all-to-all-start.1) | async-done | bytes 131104 | tf_op jit(solution)/shard_map/all_to_all | solution.py:260
  21.6 0.0 copy-start
  21.6 21.6 %all_to_all.15.stars_ref = f32[32,1,1792]{2,1,0:T(1,128)S(1)} all-to-all(f32[32,1,1792]{2,1,0:T(1,128)} %stars.1), channel_id=1, replica_groups=mesh['team'=4,'x'=4,'y'=2,'z'=8,'core'=2] {'x','z'}, dimensions={0} | all-to-all | bytes 458752 | tf_op jit(solution)/shard_map/all_to_all | solution.py:261
  43.2 0.0 copy-done
  43.2 11.6 %force.1 = f32[16,8,128]{2,1,0:T(8,128)S(1)} custom-call(f32[32,1,1792]{2,1,0:T(1,128)S(1)} %all_to_all.15.stars_ref, f32[16,16,128]{2,1,0:T(8,128)S(1)} %all-to-all-done.1.state_ref), custom_call_target="tpu_custom_call" | custom-call | tf_op jit(solution)/shard_map/force/pallas_call | solution.py:263
  54.8 12.5 %all_to_all.16.part_ref = f32[16,8,128]{2,1,0:T(8,128)} all-to-all(f32[16,8,128]{2,1,0:T(8,128)S(1)} %force.1), channel_id=1, replica_groups=mesh['team'=4,'x'=4,'y'=2,'z'=8,'core'=2] {'team','y','core'}, dimensions={0} | all-to-all | bytes 131072 | tf_op jit(solution)/shard_map/all_to_all | solution.py:278
  67.3 1.6 %correct.1 = (f32[6,128]{1,0:T(8,128)}, f32[6,128]{1,0:T(8,128)}, f32[6,128]{1,0:T(8,128)}) custom-call(f32[16,8,128]{2,1,0:T(8,128)} %all_to_all.16.part_ref, f32[16,16,128]{2,1,0:T(8,128)} %copy-done), custom_call_target="tpu_custom_call" | custom-call | tf_op jit(solution)/shard_map/correct/pallas_call | solution.py:280
Async XLA Ops:
  2.3 19.4 %all-to-all-start.1 = ((f32[16,16,128]{2,1,0:T(8,128)}), f32[16,16,128]{2,1,0:T(8,128)S(1)}, u32[]{:S(2)}, u32[]{:S(2)}) async-start(f32[16,16,128]{2,1,0:T(8,128)} %state.1), calls=%async_computation.1 | async-start | bytes 262144 | tf_op jit(solution)/shard_map/all_to_all | solution.py:260
  21.6 21.6 %copy-start = (f32[16,16,128]{2,1,0:T(8,128)}, f32[16,16,128]{2,1,0:T(8,128)S(1)}, u32[]{:S(2)}) copy-start(f32[16,16,128]{2,1,0:T(8,128)S(1)} %all-to-all-done.1.state_ref) | copy-start | bytes 393220

commit v5 on v4

--- a/solution.py
+++ b/solution.py
@@ -13,6 +13,7 @@
 REDUCE = ("team", "y", "core")
 SIDE = 256
 CYCLE = 4
+SMALL = 4 * 1024 * 1024
 F32 = jnp.float32
 BF16 = jnp.bfloat16
 
@@ -255,7 +256,10 @@
         active_slot.reshape(1, actives), active_owner.reshape(1, actives),
     )
     stars = pl.pallas_call(
-        star_kernel, out_shape=jax.ShapeDtypeStruct((n_gather, 1, 7 * members), F32), name="stars"
+        star_kernel,
+        out_shape=jax.ShapeDtypeStruct((n_gather, 1, 7 * members), F32),
+        compiler_params=pltpu.CompilerParams(vmem_limit_bytes=SMALL),
+        name="stars",
     )(position, velocity, old_accel, old_jerk, mass.reshape(1, members), elapsed)
     state = lax.all_to_all(state, REDUCE, 0, 0, tiled=True)
     stars = lax.all_to_all(stars, GATHER, 0, 0, tiled=True)
@@ -272,12 +276,17 @@
             pltpu.VMEM((members, 4 * n_act), BF16),
             pltpu.VMEM((members, LANES), F32),
         ],
-        compiler_params=pltpu.CompilerParams(vmem_limit_bytes=48 * 1024 * 1024),
+        compiler_params=pltpu.CompilerParams(vmem_limit_bytes=16 * 1024 * 1024),
         name="force",
     )(stars, state)
     part = lax.all_to_all(part, REDUCE, 0, 0, tiled=True)
     out = jax.ShapeDtypeStruct((6, actives), F32)
-    return pl.pallas_call(correct_kernel, out_shape=(out, out, out), name="correct")(part, state)
+    return pl.pallas_call(
+        correct_kernel,
+        out_shape=(out, out, out),
+        compiler_params=pltpu.CompilerParams(vmem_limit_bytes=SMALL),
+        name="correct",
+    )(part, state)
 
 
 def solution(mesh):

time: 69.3 us -> 68.1 us (0.983)
  Pallas kernels: 16.2 us -> 13.8 us
  waiting for transfers between devices: 7.73 us -> 8.49 us
    pallas_call x1, Pallas kernels: 1.48 us -> 0.03 us  [shards(): pl.pallas_call(star_kernel, out_shape=jax.ShapeDtypeStruct((n_gather, 1,...]
    pallas_call x1, Pallas kernels: 1.57 us -> 0.63 us  [shards(): pl.pallas_call(correct_kernel, out_shape=(out, out, out), compiler_params...]
    all_to_all x1, waiting for transfers between devices: 7.73 us -> 8.49 us  [shards(): state = lax.all_to_all(state, REDUCE, 0, 0, tiled=True)]
  transfers between devices with their start and end apart: 1 -> 1, of which waited for: 1 -> 1; matrix products, arithmetic and copies ran while one was open for 0% -> 0% of each run, Pallas kernels for 2% -> 0%
where the time goes in v5:
time: 68.1 us; the launch traced here: 67.8 us
  blocking collectives  33.7 us (49%)
  Pallas kernels  13.8 us (20%)
  starting transfers between devices  10.3 us (15%)
  waiting for transfers between devices  8.49 us (12%)
  between operations  0.71 us (1%)
    all_to_all x1, blocking collectives, shards(): stars = lax.all_to_all(stars, GATHER, 0, 0, tiled=True)  21.4 us
    all_to_all x1, blocking collectives, shards(): part = lax.all_to_all(part, REDUCE, 0, 0, tiled=True)  12.4 us
    pallas_call x1, Pallas kernels, shards(): pl.pallas_call(force_kernel, out_shape=jax.ShapeDtypeStruct((n_reduce, 8,...  11.6 us
    all_to_all x1, starting transfers between devices, shards(): state = lax.all_to_all(state, REDUCE, 0, 0, tiled=True)  10.3 us
    all_to_all x1, waiting for transfers between devices, shards(): state = lax.all_to_all(state, REDUCE, 0, 0, tiled=True)  8.49 us
    pallas_call x1, Pallas kernels, shards(): pl.pallas_call(state_kernel, out_shape=jax.ShapeDtypeStruct((n_reduce, 16...  1.62 us
  transfers between devices with their start and end apart: 1, of which 1 were waited for; matrix products, arithmetic and copies ran while one was open for 0% of the time, Pallas kernels for 0%

profile of v5, /device:TPU:1, one launch (start us, length us, event | category | flops | bytes accessed | tf_op | source)
XLA Modules:
  0.0 67.8 jit_solution(831093398972055681)
XLA Ops:
  0.6 1.6 %state.1 = f32[16,16,128]{2,1,0:T(8,128)} custom-call(f32[3,256]{1,0:T(4,128)} %x_ref.3, f32[3,256]{1,0:T(4,128)} %v_ref.3, f32[3,256]{1,0:T(4,128)} %a_ref.3, f32[3,256]{1,0:T(4,128)} %j_ref.3, f32[1,256]{1,0:T(1,128)} %bitcast.4, s32[1,128]{1,0:T(1,128)} %bitcast.7, s32[1,128]{1,0:T(1,128)} %bitcast.8), custom_call_target="tpu_custom_call" | custom-call | tf_op jit(solution)/shard_map/state/pallas_call | solution.py:252
  2.3 0.0 copy-start
  2.3 0.0 copy-start.1
  2.3 0.0 copy-start.2
  2.3 0.0 copy-start.3
  2.3 0.0 copy-start.5
  2.3 10.3 %all-to-all-start.1 = ((f32[16,16,128]{2,1,0:T(8,128)}), f32[16,16,128]{2,1,0:T(8,128)S(1)}, u32[]{:S(2)}, u32[]{:S(2)}) async-start(f32[16,16,128]{2,1,0:T(8,128)} %state.1), calls=%async_computation.1 | async-start | bytes 262144 | tf_op jit(solution)/shard_map/all_to_all | solution.py:264
  12.6 0.0 copy-start.4
  12.6 0.0 copy-done
  12.6 0.0 copy-done.1
  12.6 0.0 copy-done.2
  12.6 0.0 copy-done.3
  12.7 0.0 copy-done.5
  12.7 0.6 copy-done.4
  13.3 8.5 %all-to-all-done.1.state_ref = f32[16,16,128]{2,1,0:T(8,128)S(1)} async-done(((f32[16,16,128]{2,1,0:T(8,128)}), f32[16,16,128]{2,1,0:T(8,128)S(1)}, u32[]{:S(2)}, u32[]{:S(2)}) %all-to-all-start.1) | async-done | bytes 131104 | tf_op jit(solution)/shard_map/all_to_all | solution.py:264
  21.8 21.4 %all_to_all.15.stars_ref = f32[32,1,1792]{2,1,0:T(1,128)S(1)} all-to-all(f32[32,1,1792]{2,1,0:T(1,128)S(1)} %stars.1), channel_id=1, replica_groups=mesh['team'=4,'x'=4,'y'=2,'z'=8,'core'=2] {'x','z'}, dimensions={0} | all-to-all | bytes 458752 | tf_op jit(solution)/shard_map/all_to_all | solution.py:265
  43.2 11.6 %force.1 = f32[16,8,128]{2,1,0:T(8,128)S(1)} custom-call(f32[32,1,1792]{2,1,0:T(1,128)S(1)} %all_to_all.15.stars_ref, f32[16,16,128]{2,1,0:T(8,128)S(1)} %all-to-all-done.1.state_ref), custom_call_target="tpu_custom_call" | custom-call | tf_op jit(solution)/shard_map/force/pallas_call | solution.py:267
  54.8 12.4 %all_to_all.16.part_ref = f32[16,8,128]{2,1,0:T(8,128)S(1)} all-to-all(f32[16,8,128]{2,1,0:T(8,128)S(1)} %force.1), channel_id=1, replica_groups=mesh['team'=4,'x'=4,'y'=2,'z'=8,'core'=2] {'team','y','core'}, dimensions={0} | all-to-all | bytes 131072 | tf_op jit(solution)/shard_map/all_to_all | solution.py:282
  67.1 0.6 correct.1
  (1 shorter events, 0.0 us)
Async XLA Ops:
  2.3 10.4 %copy-start = (f32[3,256]{1,0:T(4,128)S(1)}, f32[3,256]{1,0:T(4,128)}, u32[]{:S(2)}) copy-start(f32[3,256]{1,0:T(4,128)} %x_ref.3) | copy-start | bytes 9220
  2.3 10.4 %copy-start.1 = (f32[3,256]{1,0:T(4,128)S(1)}, f32[3,256]{1,0:T(4,128)}, u32[]{:S(2)}) copy-start(f32[3,256]{1,0:T(4,128)} %v_ref.3) | copy-start | bytes 9220
  2.3 10.4 %copy-start.2 = (f32[3,256]{1,0:T(4,128)S(1)}, f32[3,256]{1,0:T(4,128)}, u32[]{:S(2)}) copy-start(f32[3,256]{1,0:T(4,128)} %a_ref.3) | copy-start | bytes 9220
  2.3 10.4 %copy-start.3 = (f32[3,256]{1,0:T(4,128)S(1)}, f32[3,256]{1,0:T(4,128)}, u32[]{:S(2)}) copy-start(f32[3,256]{1,0:T(4,128)} %j_ref.3) | copy-start | bytes 9220
  2.3 10.4 %copy-start.5 = (f32[256]{0:T(256)S(1)}, f32[256]{0:T(256)}, u32[]{:S(2)}) copy-start(f32[256]{0:T(256)} %param.12) | copy-start | bytes 3076
  2.3 19.5 %all-to-all-start.1 = ((f32[16,16,128]{2,1,0:T(8,128)}), f32[16,16,128]{2,1,0:T(8,128)S(1)}, u32[]{:S(2)}, u32[]{:S(2)}) async-start(f32[16,16,128]{2,1,0:T(8,128)} %state.1), calls=%async_computation.1 | async-start | bytes 262144 | tf_op jit(solution)/shard_map/all_to_all | solution.py:264
  12.6 0.7 %copy-start.4 = (f32[256]{0:T(256)S(1)}, f32[256]{0:T(256)}, u32[]{:S(2)}) copy-start(f32[256]{0:T(256)} %param.13) | copy-start | bytes 3076

commit v6 on v5

--- a/solution.py
+++ b/solution.py
@@ -14,6 +14,8 @@
 SIDE = 256
 CYCLE = 4
 SMALL = 4 * 1024 * 1024
+N_STATE = 13
+N_FORCE = 6
 F32 = jnp.float32
 BF16 = jnp.bfloat16
 
@@ -22,6 +24,15 @@
     xp = x + h * (v + h * (a / 2.0 + h * j / 6.0))
     vp = v + h * (a + h * j / 2.0)
     return (xp, vp)
+
+
+def in_line(value, count):
+    return jnp.concatenate([value[q : q + 1] for q in range(count)], axis=1)
+
+
+def in_rows(line, count):
+    width = line.shape[1] // count
+    return jnp.concatenate([line[:, q * width : (q + 1) * width] for q in range(count)], axis=0)
 
 
 def state_kernel(x_ref, v_ref, a_ref, j_ref, h_ref, slot_ref, owner_ref, state_ref):
@@ -33,8 +44,9 @@
         [x_ref[...], v_ref[...], a_ref[...], j_ref[...], h_ref[...], jnp.zeros((3, members), F32)], axis=0
     )
     chosen = jnp.dot(state, chooser, precision=lax.Precision.HIGHEST, preferred_element_type=F32)
+    line = in_line(chosen, N_STATE)
     for k in range(state_ref.shape[0]):
-        state_ref[k] = chosen
+        state_ref[k] = line
 
 
 def star_kernel(x_ref, v_ref, a_ref, j_ref, m_ref, h_ref, stars_ref):
@@ -134,6 +146,7 @@
         state = state_ref[b]
         for t in range(1, n_team):
             state = state + state_ref[t * n_blocks + b]
+        state = in_rows(state, N_STATE)
         xi, vi = predict(state[0:3], state[3:6], state[6:9], state[9:12], state[12:13])
         pack = jnp.concatenate([xi, vi, jnp.zeros((2, LANES), F32)], 0)
         at = b * LANES
@@ -215,10 +228,11 @@
     xi, vi = act_ref[0:3, :], act_ref[3:6, :]
     a = sw[0:3] - xi * sw[6:7]
     j = (sw[3:6] - vi * sw[6:7]) - 3.0 * (su[0:3] - xi * su[6:7])
-    part = jnp.concatenate([a, j, jnp.zeros((2, n_act), F32)], 0)
+    part = jnp.concatenate([a, j], 0)
     for b in range(n_blocks):
+        line = in_line(part[:, b * LANES : (b + 1) * LANES], N_FORCE)
         for t in range(n_team):
-            out_ref[t * n_blocks + b] = part[:, b * LANES : (b + 1) * LANES]
+            out_ref[t * n_blocks + b] = line
 
 
 def correct_kernel(part_ref, state_ref, phase_ref, force_ref, higher_ref):
@@ -231,6 +245,7 @@
     own = state_ref[mine]
     for t in range(1, n // n_blocks):
         own = own + state_ref[t * n_blocks + mine]
+    own, total = in_rows(own, N_STATE), in_rows(total, N_FORCE)
     x0, v0, a0, j0, dt = (own[0:3], own[3:6], own[6:9], own[9:12], own[12:13])
     a1, j1 = (total[0:3], total[3:6])
     v1 = v0 + (a0 + a1) * dt / 2.0 + (j0 - j1) * dt * dt / 12.0
@@ -250,7 +265,10 @@
     n_blocks = sizes["y"] * sizes["core"]
     elapsed = elapsed.reshape(1, members)
     state = pl.pallas_call(
-        state_kernel, out_shape=jax.ShapeDtypeStruct((n_reduce, 16, actives), F32), name="state"
+        state_kernel,
+        out_shape=jax.ShapeDtypeStruct((n_reduce, 1, N_STATE * actives), F32),
+        compiler_params=pltpu.CompilerParams(vmem_limit_bytes=SMALL),
+        name="state",
     )(
         position, velocity, old_accel, old_jerk, elapsed,
         active_slot.reshape(1, actives), active_owner.reshape(1, actives),
@@ -258,15 +276,15 @@
     stars = pl.pallas_call(
         star_kernel,
         out_shape=jax.ShapeDtypeStruct((n_gather, 1, 7 * members), F32),
-        compiler_params=pltpu.CompilerParams(vmem_limit_bytes=SMALL),
         name="stars",
     )(position, velocity, old_accel, old_jerk, mass.reshape(1, members), elapsed)
+    stars = lax.all_to_all(stars, GATHER, 0, 0, tiled=True)
+    state, stars = lax.optimization_barrier((state, stars))
     state = lax.all_to_all(state, REDUCE, 0, 0, tiled=True)
-    stars = lax.all_to_all(stars, GATHER, 0, 0, tiled=True)
     n_act = n_blocks * actives
     part = pl.pallas_call(
         force_kernel,
-        out_shape=jax.ShapeDtypeStruct((n_reduce, 8, actives), F32),
+        out_shape=jax.ShapeDtypeStruct((n_reduce, 1, N_FORCE * actives), F32),
         scratch_shapes=[
             pltpu.VMEM((LANES, 3 * n_act), BF16),
             pltpu.VMEM((8, n_act), F32),

time: 68.1 us -> 66.7 us (0.979)
  blocking collectives: 33.7 us -> 28.7 us
  starting transfers between devices: 10.3 us -> 13.9 us
    all_to_all x1, starting transfers between devices: 10.3 us -> 13.9 us  [shards(): stars = lax.all_to_all(stars, GATHER, 0, 0, tiled=True)]
    all_to_all x1, blocking collectives: 21.4 us -> 18.8 us  [shards(): state = lax.all_to_all(state, REDUCE, 0, 0, tiled=True)]
    all_to_all x1, blocking collectives: 12.4 us -> 9.88 us  [shards(): part = lax.all_to_all(part, REDUCE, 0, 0, tiled=True)]
    pallas_call x2, Pallas kernels: 13.2 us -> 11.7 us  [the longest x1 11.5 us: shards(): pl.pallas_call(force_kernel, out_shape=jax.ShapeDtypeStruct((n_reduce, 1,...]
    pallas_call x1, Pallas kernels: 0.03 us -> 1.48 us  [shards(): pl.pallas_call(star_kernel, out_shape=jax.ShapeDtypeStruct((n_gather, 1,...]
where the time goes in v6:
time: 66.7 us; the launch traced here: 66.4 us
  blocking collectives  28.7 us (43%)
  starting transfers between devices  13.9 us (21%)
  Pallas kernels  13.8 us (21%)
  waiting for transfers between devices  8.64 us (13%)
  between operations  0.73 us (1%)
    all_to_all x1, blocking collectives, shards(): state = lax.all_to_all(state, REDUCE, 0, 0, tiled=True)  18.8 us
    all_to_all x1, starting transfers between devices, shards(): stars = lax.all_to_all(stars, GATHER, 0, 0, tiled=True)  13.9 us
    pallas_call x1, Pallas kernels, shards(): pl.pallas_call(force_kernel, out_shape=jax.ShapeDtypeStruct((n_reduce, 1,...  11.5 us
    all_to_all x1, blocking collectives, shards(): part = lax.all_to_all(part, REDUCE, 0, 0, tiled=True)  9.88 us
    all_to_all x1, waiting for transfers between devices, shards(): stars = lax.all_to_all(stars, GATHER, 0, 0, tiled=True)  8.64 us
    pallas_call x1, Pallas kernels, shards(): pl.pallas_call(star_kernel, out_shape=jax.ShapeDtypeStruct((n_gather, 1,...  1.48 us
  transfers between devices with their start and end apart: 1, of which 1 were waited for; matrix products, arithmetic and copies ran while one was open for 0% of the time, Pallas kernels for 0%

profile of v6, /device:TPU:1, one launch (start us, length us, event | category | flops | bytes accessed | tf_op | source)
XLA Modules:
  0.0 66.4 jit_solution(106489131316811961)
XLA Ops:
  0.6 1.5 %stars.1 = f32[32,1,1792]{2,1,0:T(1,128)} custom-call(f32[3,256]{1,0:T(4,128)} %x_ref.3, f32[3,256]{1,0:T(4,128)} %v_ref.3, f32[3,256]{1,0:T(4,128)} %a_ref.3, f32[3,256]{1,0:T(4,128)} %j_ref.3, f32[1,256]{1,0:T(1,128)} %bitcast.8, f32[1,256]{1,0:T(1,128)} %bitcast.4), custom_call_target="tpu_custom_call" | custom-call | tf_op jit(solution)/shard_map/stars/pallas_call | solution.py:276
  2.1 0.0 copy-start
  2.1 0.0 copy-start.1
  2.1 0.0 copy-start.2
  2.1 0.0 copy-start.3
  2.1 0.0 copy-start.6
  2.1 13.9 %all-to-all-start = ((f32[32,1,1792]{2,1,0:T(1,128)}), f32[32,1,1792]{2,1,0:T(1,128)S(1)}, u32[]{:S(2)}, u32[]{:S(2)}) async-start(f32[32,1,1792]{2,1,0:T(1,128)} %stars.1), calls=%async_computation | async-start | bytes 458752 | tf_op jit(solution)/shard_map/all_to_all | solution.py:281
  16.0 0.0 copy-start.4
  16.0 0.0 copy-start.5
  16.0 0.0 copy-done
  16.0 0.0 copy-done.1
  16.1 0.0 copy-done.2
  16.1 0.0 copy-done.3
  16.1 0.0 copy-done.6
  16.1 0.6 copy-done.4
  16.7 0.0 copy-done.5
  16.7 0.2 state.1
  16.9 8.6 %all-to-all-done.stars_ref = f32[32,1,1792]{2,1,0:T(1,128)S(1)} async-done(((f32[32,1,1792]{2,1,0:T(1,128)}), f32[32,1,1792]{2,1,0:T(1,128)S(1)}, u32[]{:S(2)}, u32[]{:S(2)}) %all-to-all-start) | async-done | bytes 229408 | tf_op jit(solution)/shard_map/all_to_all | solution.py:281
  25.6 18.8 %all_to_all.15.state_ref = f32[16,1,1664]{2,1,0:T(1,128)S(1)} all-to-all(f32[16,1,1664]{2,1,0:T(1,128)S(1)} %state.1), channel_id=1, replica_groups=mesh['team'=4,'x'=4,'y'=2,'z'=8,'core'=2] {'team','y','core'}, dimensions={0} | all-to-all | bytes 212992 | tf_op jit(solution)/shard_map/all_to_all | solution.py:283
  44.4 11.5 %force.1 = f32[16,1,768]{2,1,0:T(1,128)S(1)} custom-call(f32[32,1,1792]{2,1,0:T(1,128)S(1)} %all-to-all-done.stars_ref, f32[16,1,1664]{2,1,0:T(1,128)S(1)} %all_to_all.15.state_ref), custom_call_target="tpu_custom_call" | custom-call | tf_op jit(solution)/shard_map/force/pallas_call | solution.py:285
  55.9 9.9 %all_to_all.16.part_ref = f32[16,1,768]{2,1,0:T(1,128)S(1)} all-to-all(f32[16,1,768]{2,1,0:T(1,128)S(1)} %force.1), channel_id=1, replica_groups=mesh['team'=4,'x'=4,'y'=2,'z'=8,'core'=2] {'team','y','core'}, dimensions={0} | all-to-all | bytes 98304 | tf_op jit(solution)/shard_map/all_to_all | solution.py:300
  65.8 0.6 correct.1
Async XLA Ops:
  2.1 13.9 %copy-start = (f32[3,256]{1,0:T(4,128)S(1)}, f32[3,256]{1,0:T(4,128)}, u32[]{:S(2)}) copy-start(f32[3,256]{1,0:T(4,128)} %x_ref.3) | copy-start | bytes 9220
  2.1 13.9 %copy-start.1 = (f32[3,256]{1,0:T(4,128)S(1)}, f32[3,256]{1,0:T(4,128)}, u32[]{:S(2)}) copy-start(f32[3,256]{1,0:T(4,128)} %v_ref.3) | copy-start | bytes 9220
  2.1 13.9 %copy-start.2 = (f32[3,256]{1,0:T(4,128)S(1)}, f32[3,256]{1,0:T(4,128)}, u32[]{:S(2)}) copy-start(f32[3,256]{1,0:T(4,128)} %a_ref.3) | copy-start | bytes 9220
  2.1 13.9 %copy-start.3 = (f32[3,256]{1,0:T(4,128)S(1)}, f32[3,256]{1,0:T(4,128)}, u32[]{:S(2)}) copy-start(f32[3,256]{1,0:T(4,128)} %j_ref.3) | copy-start | bytes 9220
  2.1 13.9 %copy-start.6 = (s32[128]{0:T(128)S(1)}, s32[128]{0:T(128)}, u32[]{:S(2)}) copy-start(s32[128]{0:T(128)} %param.15) | copy-start | bytes 1540
  2.1 23.4 %all-to-all-start = ((f32[32,1,1792]{2,1,0:T(1,128)}), f32[32,1,1792]{2,1,0:T(1,128)S(1)}, u32[]{:S(2)}, u32[]{:S(2)}) async-start(f32[32,1,1792]{2,1,0:T(1,128)} %stars.1), calls=%async_computation | async-start | bytes 458752 | tf_op jit(solution)/shard_map/all_to_all | solution.py:281
  16.0 0.7 %copy-start.4 = (f32[256]{0:T(256)S(1)}, f32[256]{0:T(256)}, u32[]{:S(2)}) copy-start(f32[256]{0:T(256)} %param.13) | copy-start | bytes 3076
  16.0 0.7 %copy-start.5 = (s32[128]{0:T(128)S(1)}, s32[128]{0:T(128)}, u32[]{:S(2)}) copy-start(s32[128]{0:T(128)} %param.14) | copy-start | bytes 1540

commit v7 on v6

--- a/solution.py
+++ b/solution.py
@@ -135,7 +135,9 @@
     return jnp.concatenate(pieces(heavy), 0).astype(BF16)
 
 
-def force_kernel(stars_ref, state_ref, out_ref, met_ref, act_ref, sum_ref, feat_ref, prod_ref, weight_ref, col_ref):
+def force_kernel(
+    stars_ref, state_ref, slot_ref, owner_ref, out_ref, met_ref, act_ref, mid_ref, sum_ref, feat_ref, prod_ref, weight_ref, col_ref
+):
     n_tiles = stars_ref.shape[0]
     n_blocks = N_YLO * N_CORE
     n_team = state_ref.shape[0] // n_blocks
@@ -149,7 +151,13 @@
         state = in_rows(state, N_STATE)
         xi, vi = predict(state[0:3], state[3:6], state[6:9], state[9:12], state[12:13])
         pack = jnp.concatenate([xi, vi, jnp.zeros((2, LANES), F32)], 0)
+        act_ref[:, b * LANES : (b + 1) * LANES] = pack
+
+    mean = jnp.sum(act_ref[...], axis=1, keepdims=True) * (1.0 / n_act)
+    mid_ref[...] = jnp.broadcast_to(jnp.round(mean * 2.0) * 0.5, mid_ref.shape)
+    for b in range(n_blocks):
         at = b * LANES
+        pack = act_ref[:, at : at + LANES] - mid_ref[:, :LANES]
         act_ref[:, at : at + LANES] = pack
         for k, rows in enumerate(active_rows(pack)):
             met_ref[:, k * n_act + at : k * n_act + at + LANES] = rows.astype(BF16)
@@ -158,7 +166,7 @@
         line = stars_ref[t]
         members = line.shape[1] // 7
         rows = [line[:, q * members : (q + 1) * members] for q in range(7)]
-        return jnp.concatenate(rows + [jnp.zeros((1, members), F32)], 0)
+        return jnp.concatenate(rows + [jnp.zeros((1, members), F32)], 0) - mid_ref[...]
 
     def on_matrix(tile, side):
         return side < n_act // 2 or tile % CYCLE != CYCLE - 1
@@ -176,7 +184,7 @@
                 feat_ref[...], met_ref[:, at : at + SIDE], preferred_element_type=F32
             )
 
-    def weights(side, tile):
+    def weights(side, tile, same=None):
         cross = prod_ref[:, 2 * n_act + side : 2 * n_act + side + SIDE]
         if on_matrix(tile, side):
             r2 = prod_ref[:, side : side + SIDE] + prod_ref[:, n_act + side : n_act + side + SIDE]
@@ -188,6 +196,8 @@
         inv2 = inv * inv
         w = inv * inv2
         u = w * inv2 * cross
+        if same is not None:
+            w, u = (jnp.where(same[:, side : side + SIDE], 0.0, value) for value in (w, u))
         for k, value in enumerate((w, u)):
             upper = value.astype(BF16)
             at = 2 * k * n_act + side
@@ -205,7 +215,19 @@
             at = k * n_act + side
             sum_ref[:, at : at + SIDE] = sum_ref[:, at : at + SIDE] + part
 
+    here = lax.axis_index("x") * N_Z + lax.axis_index("z")
+    mine = lax.axis_index("y") * N_CORE + lax.axis_index("core")
+    wanted = jnp.where(owner_ref[...] == lax.axis_index("team"), slot_ref[...], -1)
+    wanted = jnp.concatenate([jnp.where(mine == b, wanted, -1) for b in range(n_blocks)], 1)
     sum_ref[...] = jnp.zeros_like(sum_ref)
+    prepare(here, 0)
+    for side in sides:
+        products(side, 0)
+    same = lax.broadcasted_iota(jnp.int32, (feat_ref.shape[0], n_act), 0) == wanted
+    heavy = heavy_rows(block_of(here))
+    for side in sides:
+        weights(side, 0, same)
+        add_up(heavy, side)
     prepare(0, 0)
     for side in sides:
         products(side, 0)
@@ -214,7 +236,7 @@
     def one_cycle(c, _):
         for tile in range(CYCLE):
             t = c * CYCLE + tile
-            heavy = heavy_rows(block_of(t))
+            heavy = heavy_rows(block_of(t)) * (t != here).astype(BF16)
             for side in sides:
                 weights(side, tile)
                 products(side, tile + 1)
@@ -288,6 +310,7 @@
         scratch_shapes=[
             pltpu.VMEM((LANES, 3 * n_act), BF16),
             pltpu.VMEM((8, n_act), F32),
+            pltpu.VMEM((8, members), F32),
             pltpu.VMEM((24, 2 * n_act), F32),
             pltpu.VMEM((members, LANES), BF16),
             pltpu.VMEM((members, 3 * n_act), F32),
@@ -296,7 +319,7 @@
         ],
         compiler_params=pltpu.CompilerParams(vmem_limit_bytes=16 * 1024 * 1024),
         name="force",
-    )(stars, state)
+    )(stars, state, active_slot.reshape(1, actives), active_owner.reshape(1, actives))
     part = lax.all_to_all(part, REDUCE, 0, 0, tiled=True)
     out = jax.ShapeDtypeStruct((6, actives), F32)
     return pl.pallas_call(

time: 66.7 us -> 69.5 us (1.042)
  Pallas kernels: 13.8 us -> 16.6 us
    pallas_call x1, Pallas kernels: 11.5 us -> 14.3 us  [shards(): pl.pallas_call(force_kernel, out_shape=jax.ShapeDtypeStruct((n_reduce, 1,...]
where the time goes in v7:
time: 69.5 us; the launch traced here: 69.2 us
  blocking collectives  28.7 us (41%)
  Pallas kernels  16.6 us (24%)
  starting transfers between devices  13.9 us (20%)
  waiting for transfers between devices  8.64 us (12%)
  between operations  0.73 us (1%)
    all_to_all x1, blocking collectives, shards(): state = lax.all_to_all(state, REDUCE, 0, 0, tiled=True)  18.8 us
    pallas_call x1, Pallas kernels, shards(): pl.pallas_call(force_kernel, out_shape=jax.ShapeDtypeStruct((n_reduce, 1,...  14.3 us
    all_to_all x1, starting transfers between devices, shards(): stars = lax.all_to_all(stars, GATHER, 0, 0, tiled=True)  13.9 us
    all_to_all x1, blocking collectives, shards(): part = lax.all_to_all(part, REDUCE, 0, 0, tiled=True)  9.9 us
    all_to_all x1, waiting for transfers between devices, shards(): stars = lax.all_to_all(stars, GATHER, 0, 0, tiled=True)  8.64 us
    pallas_call x1, Pallas kernels, shards(): pl.pallas_call(star_kernel, out_shape=jax.ShapeDtypeStruct((n_gather, 1,...  1.48 us
  transfers between devices with their start and end apart: 1, of which 1 were waited for; matrix products, arithmetic and copies ran while one was open for 0% of the time, Pallas kernels for 0%

profile of v7, /device:TPU:1, one launch (start us, length us, event | category | flops | bytes accessed | tf_op | source)
XLA Modules:
  0.0 69.2 jit_solution(2332404165947703982)
XLA Ops:
  0.6 1.5 %stars.1 = f32[32,1,1792]{2,1,0:T(1,128)} custom-call(f32[3,256]{1,0:T(4,128)} %x_ref.3, f32[3,256]{1,0:T(4,128)} %v_ref.3, f32[3,256]{1,0:T(4,128)} %a_ref.3, f32[3,256]{1,0:T(4,128)} %j_ref.3, f32[1,256]{1,0:T(1,128)} %bitcast.10, f32[1,256]{1,0:T(1,128)} %bitcast.4), custom_call_target="tpu_custom_call" | custom-call | tf_op jit(solution)/shard_map/stars/pallas_call | solution.py:298
  2.1 0.0 copy-start
  2.1 0.0 copy-start.1
  2.1 0.0 copy-start.2
  2.1 0.0 copy-start.3
  2.1 0.0 copy-start.6
  2.1 13.9 %all-to-all-start = ((f32[32,1,1792]{2,1,0:T(1,128)}), f32[32,1,1792]{2,1,0:T(1,128)S(1)}, u32[]{:S(2)}, u32[]{:S(2)}) async-start(f32[32,1,1792]{2,1,0:T(1,128)} %stars.1), calls=%async_computation | async-start | bytes 458752 | tf_op jit(solution)/shard_map/all_to_all | solution.py:303
  16.0 0.0 copy-start.4
  16.0 0.0 copy-start.5
  16.0 0.0 copy-done
  16.0 0.0 copy-done.1
  16.1 0.0 copy-done.2
  16.1 0.0 copy-done.3
  16.1 0.0 copy-done.6
  16.1 0.6 copy-done.4
  16.7 0.0 copy-done.5
  16.7 0.2 state.1
  16.9 8.6 %all-to-all-done.stars_ref = f32[32,1,1792]{2,1,0:T(1,128)S(1)} async-done(((f32[32,1,1792]{2,1,0:T(1,128)}), f32[32,1,1792]{2,1,0:T(1,128)S(1)}, u32[]{:S(2)}, u32[]{:S(2)}) %all-to-all-start) | async-done | bytes 229408 | tf_op jit(solution)/shard_map/all_to_all | solution.py:303
  25.6 18.8 %all_to_all.15.state_ref = f32[16,1,1664]{2,1,0:T(1,128)S(1)} all-to-all(f32[16,1,1664]{2,1,0:T(1,128)S(1)} %state.1), channel_id=1, replica_groups=mesh['team'=4,'x'=4,'y'=2,'z'=8,'core'=2] {'team','y','core'}, dimensions={0} | all-to-all | bytes 212992 | tf_op jit(solution)/shard_map/all_to_all | solution.py:305
  44.4 14.3 %force.1 = f32[16,1,768]{2,1,0:T(1,128)S(1)} custom-call(f32[32,1,1792]{2,1,0:T(1,128)S(1)} %all-to-all-done.stars_ref, f32[16,1,1664]{2,1,0:T(1,128)S(1)} %all_to_all.15.state_ref, s32[1,128]{1,0:T(1,128)S(1)} %bitcast.7, s32[1,128]{1,0:T(1,128)S(1)} %bitcast.9), custom_call_target="tpu_custom_call" | custom-call | tf_op jit(solution)/shard_map/force/pallas_call | solution.py:307
  58.6 9.9 %all_to_all.16.part_ref = f32[16,1,768]{2,1,0:T(1,128)S(1)} all-to-all(f32[16,1,768]{2,1,0:T(1,128)S(1)} %force.1), channel_id=1, replica_groups=mesh['team'=4,'x'=4,'y'=2,'z'=8,'core'=2] {'team','y','core'}, dimensions={0} | all-to-all | bytes 98304 | tf_op jit(solution)/shard_map/all_to_all | solution.py:323
  68.5 0.6 correct.1
Async XLA Ops:
  2.1 13.9 %copy-start = (f32[3,256]{1,0:T(4,128)S(1)}, f32[3,256]{1,0:T(4,128)}, u32[]{:S(2)}) copy-start(f32[3,256]{1,0:T(4,128)} %x_ref.3) | copy-start | bytes 9220
  2.1 13.9 %copy-start.1 = (f32[3,256]{1,0:T(4,128)S(1)}, f32[3,256]{1,0:T(4,128)}, u32[]{:S(2)}) copy-start(f32[3,256]{1,0:T(4,128)} %v_ref.3) | copy-start | bytes 9220
  2.1 13.9 %copy-start.2 = (f32[3,256]{1,0:T(4,128)S(1)}, f32[3,256]{1,0:T(4,128)}, u32[]{:S(2)}) copy-start(f32[3,256]{1,0:T(4,128)} %a_ref.3) | copy-start | bytes 9220
  2.1 13.9 %copy-start.3 = (f32[3,256]{1,0:T(4,128)S(1)}, f32[3,256]{1,0:T(4,128)}, u32[]{:S(2)}) copy-start(f32[3,256]{1,0:T(4,128)} %j_ref.3) | copy-start | bytes 9220
  2.1 13.9 %copy-start.6 = (s32[128]{0:T(128)S(1)}, s32[128]{0:T(128)}, u32[]{:S(2)}) copy-start(s32[128]{0:T(128)} %param.15) | copy-start | bytes 1540
  2.1 23.4 %all-to-all-start = ((f32[32,1,1792]{2,1,0:T(1,128)}), f32[32,1,1792]{2,1,0:T(1,128)S(1)}, u32[]{:S(2)}, u32[]{:S(2)}) async-start(f32[32,1,1792]{2,1,0:T(1,128)} %stars.1), calls=%async_computation | async-start | bytes 458752 | tf_op jit(solution)/shard_map/all_to_all | solution.py:303
  16.0 0.7 copy-start.4
  16.0 0.7 copy-start.5

commit v8 on v7

--- a/solution.py
+++ b/solution.py
@@ -220,28 +220,28 @@
     wanted = jnp.where(owner_ref[...] == lax.axis_index("team"), slot_ref[...], -1)
     wanted = jnp.concatenate([jnp.where(mine == b, wanted, -1) for b in range(n_blocks)], 1)
     sum_ref[...] = jnp.zeros_like(sum_ref)
-    prepare(here, 0)
+
+    def nth(t):
+        return lax.rem(here + t, n_tiles)
+
+    prepare(nth(0), 0)
     for side in sides:
         products(side, 0)
-    same = lax.broadcasted_iota(jnp.int32, (feat_ref.shape[0], n_act), 0) == wanted
-    heavy = heavy_rows(block_of(here))
-    for side in sides:
-        weights(side, 0, same)
-        add_up(heavy, side)
-    prepare(0, 0)
-    for side in sides:
-        products(side, 0)
-    prepare(1, 1)
+    prepare(nth(1), 1)
 
     def one_cycle(c, _):
         for tile in range(CYCLE):
             t = c * CYCLE + tile
-            heavy = heavy_rows(block_of(t)) * (t != here).astype(BF16)
+            heavy = heavy_rows(block_of(nth(t)))
+            same = None
+            if tile == 0:
+                star = lax.broadcasted_iota(jnp.int32, (feat_ref.shape[0], n_act), 0)
+                same = star == jnp.where(c == 0, wanted, -1)
             for side in sides:
-                weights(side, tile)
+                weights(side, tile, same)
                 products(side, tile + 1)
                 add_up(heavy, side)
-            prepare(jnp.minimum(t + 2, n_tiles - 1), tile + 2)
+            prepare(nth(jnp.minimum(t + 2, n_tiles - 1)), tile + 2)
         return 0
 
     lax.fori_loop(0, n_tiles // CYCLE, one_cycle, 0, unroll=2)

time: 69.5 us -> 68.1 us (0.980)
  Pallas kernels: 16.6 us -> 15.2 us
    pallas_call x1, Pallas kernels: 14.3 us -> 12.9 us  [shards(): pl.pallas_call(force_kernel, out_shape=jax.ShapeDtypeStruct((n_reduce, 1,...]
where the time goes in v8:
time: 68.1 us; the launch traced here: 67.8 us
  blocking collectives  28.7 us (42%)
  Pallas kernels  15.2 us (22%)
  starting transfers between devices  13.9 us (20%)
  waiting for transfers between devices  8.64 us (13%)
  between operations  0.73 us (1%)
    all_to_all x1, blocking collectives, shards(): state = lax.all_to_all(state, REDUCE, 0, 0, tiled=True)  18.8 us
    all_to_all x1, starting transfers between devices, shards(): stars = lax.all_to_all(stars, GATHER, 0, 0, tiled=True)  13.9 us
    pallas_call x1, Pallas kernels, shards(): pl.pallas_call(force_kernel, out_shape=jax.ShapeDtypeStruct((n_reduce, 1,...  12.9 us
    all_to_all x1, blocking collectives, shards(): part = lax.all_to_all(part, REDUCE, 0, 0, tiled=True)  9.88 us
    all_to_all x1, waiting for transfers between devices, shards(): stars = lax.all_to_all(stars, GATHER, 0, 0, tiled=True)  8.64 us
    pallas_call x1, Pallas kernels, shards(): pl.pallas_call(star_kernel, out_shape=jax.ShapeDtypeStruct((n_gather, 1,...  1.48 us
  transfers between devices with their start and end apart: 1, of which 1 were waited for; matrix products, arithmetic and copies ran while one was open for 0% of the time, Pallas kernels for 0%

profile of v8, /device:TPU:1, one launch (start us, length us, event | category | flops | bytes accessed | tf_op | source)
XLA Modules:
  0.0 67.8 jit_solution(18324386061889273156)
XLA Ops:
  0.6 1.5 %stars.1 = f32[32,1,1792]{2,1,0:T(1,128)} custom-call(f32[3,256]{1,0:T(4,128)} %x_ref.3, f32[3,256]{1,0:T(4,128)} %v_ref.3, f32[3,256]{1,0:T(4,128)} %a_ref.3, f32[3,256]{1,0:T(4,128)} %j_ref.3, f32[1,256]{1,0:T(1,128)} %bitcast.10, f32[1,256]{1,0:T(1,128)} %bitcast.4), custom_call_target="tpu_custom_call" | custom-call | tf_op jit(solution)/shard_map/stars/pallas_call | solution.py:298
  2.1 0.0 copy-start
  2.1 0.0 copy-start.1
  2.1 0.0 copy-start.2
  2.1 0.0 copy-start.3
  2.1 0.0 copy-start.6
  2.1 13.9 %all-to-all-start = ((f32[32,1,1792]{2,1,0:T(1,128)}), f32[32,1,1792]{2,1,0:T(1,128)S(1)}, u32[]{:S(2)}, u32[]{:S(2)}) async-start(f32[32,1,1792]{2,1,0:T(1,128)} %stars.1), calls=%async_computation | async-start | bytes 458752 | tf_op jit(solution)/shard_map/all_to_all | solution.py:303
  16.0 0.0 copy-start.4
  16.0 0.0 copy-start.5
  16.0 0.0 copy-done
  16.0 0.0 copy-done.1
  16.1 0.0 copy-done.2
  16.1 0.0 copy-done.3
  16.1 0.0 copy-done.6
  16.1 0.6 copy-done.4
  16.7 0.0 copy-done.5
  16.7 0.2 state.1
  16.9 8.6 %all-to-all-done.stars_ref = f32[32,1,1792]{2,1,0:T(1,128)S(1)} async-done(((f32[32,1,1792]{2,1,0:T(1,128)}), f32[32,1,1792]{2,1,0:T(1,128)S(1)}, u32[]{:S(2)}, u32[]{:S(2)}) %all-to-all-start) | async-done | bytes 229408 | tf_op jit(solution)/shard_map/all_to_all | solution.py:303
  25.6 18.8 %all_to_all.15.state_ref = f32[16,1,1664]{2,1,0:T(1,128)S(1)} all-to-all(f32[16,1,1664]{2,1,0:T(1,128)S(1)} %state.1), channel_id=1, replica_groups=mesh['team'=4,'x'=4,'y'=2,'z'=8,'core'=2] {'team','y','core'}, dimensions={0} | all-to-all | bytes 212992 | tf_op jit(solution)/shard_map/all_to_all | solution.py:305
  44.4 12.9 %force.1 = f32[16,1,768]{2,1,0:T(1,128)S(1)} custom-call(f32[32,1,1792]{2,1,0:T(1,128)S(1)} %all-to-all-done.stars_ref, f32[16,1,1664]{2,1,0:T(1,128)S(1)} %all_to_all.15.state_ref, s32[1,128]{1,0:T(1,128)S(1)} %bitcast.7, s32[1,128]{1,0:T(1,128)S(1)} %bitcast.9), custom_call_target="tpu_custom_call" | custom-call | tf_op jit(solution)/shard_map/force/pallas_call | solution.py:307
  57.3 9.9 %all_to_all.16.part_ref = f32[16,1,768]{2,1,0:T(1,128)S(1)} all-to-all(f32[16,1,768]{2,1,0:T(1,128)S(1)} %force.1), channel_id=1, replica_groups=mesh['team'=4,'x'=4,'y'=2,'z'=8,'core'=2] {'team','y','core'}, dimensions={0} | all-to-all | bytes 98304 | tf_op jit(solution)/shard_map/all_to_all | solution.py:323
  67.2 0.6 correct.1
Async XLA Ops:
  2.1 13.9 %copy-start = (f32[3,256]{1,0:T(4,128)S(1)}, f32[3,256]{1,0:T(4,128)}, u32[]{:S(2)}) copy-start(f32[3,256]{1,0:T(4,128)} %x_ref.3) | copy-start | bytes 9220
  2.1 13.9 %copy-start.1 = (f32[3,256]{1,0:T(4,128)S(1)}, f32[3,256]{1,0:T(4,128)}, u32[]{:S(2)}) copy-start(f32[3,256]{1,0:T(4,128)} %v_ref.3) | copy-start | bytes 9220
  2.1 13.9 %copy-start.2 = (f32[3,256]{1,0:T(4,128)S(1)}, f32[3,256]{1,0:T(4,128)}, u32[]{:S(2)}) copy-start(f32[3,256]{1,0:T(4,128)} %a_ref.3) | copy-start | bytes 9220
  2.1 13.9 %copy-start.3 = (f32[3,256]{1,0:T(4,128)S(1)}, f32[3,256]{1,0:T(4,128)}, u32[]{:S(2)}) copy-start(f32[3,256]{1,0:T(4,128)} %j_ref.3) | copy-start | bytes 9220
  2.1 13.9 %copy-start.6 = (s32[128]{0:T(128)S(1)}, s32[128]{0:T(128)}, u32[]{:S(2)}) copy-start(s32[128]{0:T(128)} %param.15) | copy-start | bytes 1540
  2.1 23.4 %all-to-all-start = ((f32[32,1,1792]{2,1,0:T(1,128)}), f32[32,1,1792]{2,1,0:T(1,128)S(1)}, u32[]{:S(2)}, u32[]{:S(2)}) async-start(f32[32,1,1792]{2,1,0:T(1,128)} %stars.1), calls=%async_computation | async-start | bytes 458752 | tf_op jit(solution)/shard_map/all_to_all | solution.py:303
  16.0 0.7 %copy-start.4 = (f32[256]{0:T(256)S(1)}, f32[256]{0:T(256)}, u32[]{:S(2)}) copy-start(f32[256]{0:T(256)} %param.13) | copy-start | bytes 3076
  16.0 0.7 copy-start.5
